TPU v7x, 128 devices: a whole 4x4x4 slice. The times are simulated.
128 devices in a mesh: dp: 64 (over y_hi, x, z, core), tensor: 2 (over y_lo).
Axes of the slice: x: 4, y: 4 (y_hi: 2, y_lo: 2; y = y_hi * 2 + y_lo), z: 4, core: 2. Of those that a mesh axis runs over, the one named last changes fastest.
Arguments:
- tokens_in: bfloat16 [32768, 1536], P(('dp', 'tensor')), may hold values from -6 to 6
- routes: int32 [32768, 4], P('dp'), may hold values from 0 to 7, all different within a row; in each aligned block of 512 rows (0 to 511, 512 to 1023, ...) at most 320 rows name the same one
- cotangent: bfloat16 [32768, 1536], P(('dp', 'tensor')), may hold values from -6 to 6
- attn_gain: bfloat16 [1536], P('dp'), may hold values from 0.5 to 1.5
- query_proj: bfloat16 [1536, 1536], P('dp', 'tensor'), may hold values from -0.15625 to 0.15625
- key_proj: bfloat16 [1536, 256], P('dp', 'tensor'), may hold values from -0.15625 to 0.15625
- value_proj: bfloat16 [1536, 256], P('dp', 'tensor'), may hold values from -0.15625 to 0.15625
- output_proj: bfloat16 [1536, 1536], P('dp', 'tensor'), may hold values from -0.625 to 0.625
- ffn_gain: bfloat16 [1536], P('dp'), may hold values from 0.5 to 1.5
- router_proj: bfloat16 [1536, 8], P('dp'), may hold values from -0.078125 to 0.078125
- expert_gate: bfloat16 [1536, 8, 768], P('dp', None, 'tensor'), may hold values from -0.15625 to 0.15625
- expert_up: bfloat16 [1536, 8, 768], P('dp', None, 'tensor'), may hold values from -0.15625 to 0.15625
- expert_down: bfloat16 [1536, 8, 768], P('dp', None, 'tensor'), may hold values from -0.4375 to 0.4375
Outputs:
- layer_output: bfloat16 [32768, 1536], P(('dp', 'tensor'))
- grad_input: bfloat16 [32768, 1536], P(('dp', 'tensor'))
- grad_attn_gain: float32 [1536], P(('dp', 'tensor'))
- grad_query: float32 [1536, 1536], P('dp', 'tensor')
- grad_key: float32 [1536, 256], P('dp', 'tensor')
- grad_value: float32 [1536, 256], P('dp', 'tensor')
- grad_output_proj: float32 [1536, 1536], P('dp', 'tensor')
- grad_ffn_gain: float32 [1536], P(('dp', 'tensor'))
- grad_router: float32 [1536, 8], P(('dp', 'tensor'))
- grad_expert_gate: float32 [1536, 8, 768], P('dp', None, 'tensor')
- grad_expert_up: float32 [1536, 8, 768], P('dp', None, 'tensor')
- grad_expert_down: float32 [1536, 8, 768], P('dp', None, 'tensor')
Inputs may be any that keep to these rules, and one draw needn't show every extreme that they name: `routes`: each row names 4 different experts; in each aligned block of 512 rows (one sequence) no expert is named by more than 320 rows, and one is named by exactly 320.
All inputs are finite; a program needn't handle non-finite values.
Results may differ from a plain program's by a relative error of at most 0.02.
Values may be sent and summed in bfloat16 or wider, within the bound.
A program may use at most 256 MiB of HBM per device.

v0:
```python
import jax
import jax.numpy as jnp
from jax import lax
from jax.sharding import PartitionSpec as P

HD = 128
E = 8
TOP = 4
CAP = 320


NORM_EPSILON = 1e-06
ROPE_BASE = 1000000.0
HIGHEST_MODE = lax.Precision.HIGHEST


def rope_tables(length, head_size):
    half_size = head_size // 2
    frequency = ROPE_BASE ** (-(2.0 * jnp.arange(half_size, dtype=jnp.float32)) / head_size)
    angles = jnp.arange(length, dtype=jnp.float32)[:, None] * frequency[None, :]
    angles = jnp.concatenate([angles, angles], axis=1)
    return (jnp.cos(angles), jnp.sin(angles))


def rotate(values, cosine, sine_table):
    half_size = values.shape[-1] // 2
    turned = jnp.concatenate([-values[..., half_size:], values[..., :half_size]], axis=-1)
    return values * cosine[:, None, :] + turned * sine_table[:, None, :]


def unrotate(gradient, cosine, sine_table):
    half_size = gradient.shape[-1] // 2
    carried = gradient * sine_table[:, None, :]
    turned = jnp.concatenate([-carried[..., half_size:], carried[..., :half_size]], axis=-1)
    return gradient * cosine[:, None, :] - turned


def norm_forward(tokens, gain_vec):
    inverse = lax.rsqrt(jnp.mean(tokens * tokens, axis=1, keepdims=True) + NORM_EPSILON)
    return (tokens * inverse * gain_vec, inverse)


def norm_backward(tokens, inverse, gain_vec, gradient):
    scaled = gradient * gain_vec
    gain_grad = jnp.sum(gradient * tokens * inverse, axis=0)
    token_grad = inverse * scaled - tokens * inverse**3 * jnp.mean(
        scaled * tokens, axis=1, keepdims=True
    )
    return (token_grad, gain_grad)


def block_scores(query_block, keys, first_row, head_scale):
    block_rows = query_block.shape[0]
    length = keys.shape[0]
    scores = (
        jnp.einsum("qkgd,skd->kgqs", query_block, keys, preferred_element_type=jnp.float32)
        * head_scale
    )
    allowed = (first_row + jnp.arange(block_rows))[:, None] >= jnp.arange(length)[None, :]
    return jnp.where(allowed, scores, -1e30)


def attend(queries, keys, values):
    length, kv_local, head_size = keys.shape
    group_size = queries.shape[1] // kv_local
    block_rows = min(512, length)
    grouped = queries.reshape(length, kv_local, group_size, head_size)
    head_scale = head_size ** (-0.5)

    def one_block(block_index):
        first_row = block_index * block_rows
        scores = block_scores(grouped, keys, first_row, head_scale)
        row_max = jnp.max(scores, axis=-1, keepdims=True)
        shifted = jnp.exp(scores - row_max)
        row_total = jnp.sum(shifted, axis=-1, keepdims=True)
        attn_probs = (shifted / row_total).astype(jnp.bfloat16)
        mixed_out = jnp.einsum(
            "kgqs,skd->qkgd", attn_probs, values, preferred_element_type=jnp.float32
        )
        return (mixed_out.astype(jnp.bfloat16), (row_max + jnp.log(row_total))[..., 0])

    attended, log_total = lax.map(one_block, jnp.arange(length // block_rows))
    return (attended.reshape(length, kv_local * group_size * head_size), log_total)


def attend_back(queries, keys, values, log_total, grad_attended):
    length, kv_local, head_size = keys.shape
    group_size = queries.shape[1] // kv_local
    block_rows = min(512, length)
    grouped = queries.reshape(length, kv_local, group_size, head_size)
    grad_grouped = grad_attended.reshape(length, kv_local, group_size, head_size)
    head_scale = head_size ** (-0.5)

    def one_block(totals, block_index):
        key_total, value_total = totals
        first_row = block_index * block_rows
        scores = block_scores(grouped, keys, first_row, head_scale)
        attn_probs = jnp.exp(scores - log_total[block_index][..., None])
        probs_low = attn_probs.astype(jnp.bfloat16)
        grad_probs = jnp.einsum(
            "qkgd,skd->kgqs", grad_grouped, values, preferred_element_type=jnp.float32
        )
        centred = jnp.sum(attn_probs * grad_probs, axis=-1, keepdims=True)
        grad_scores = (attn_probs * (grad_probs - centred)).astype(jnp.bfloat16)
        grad_query = (
            jnp.einsum("kgqs,skd->qkgd", grad_scores, keys, preferred_element_type=jnp.float32)
            * head_scale
        )
        key_total = (
            key_total
            + jnp.einsum("kgqs,qkgd->skd", grad_scores, grouped, preferred_element_type=jnp.float32)
            * head_scale
        )
        value_total = value_total + jnp.einsum(
            "kgqs,qkgd->skd", probs_low, grad_grouped, preferred_element_type=jnp.float32
        )
        return ((key_total, value_total), grad_query)

    zero_heads = jnp.zeros((length, kv_local, head_size), jnp.float32)
    (grad_keys, grad_values), grad_queries = lax.scan(
        one_block, (zero_heads, zero_heads), jnp.arange(length // block_rows)
    )
    return (grad_queries.reshape(length, kv_local * group_size, head_size), grad_keys, grad_values)


def shards(
    tokens_in,
    routes,
    cotangent,
    attn_gain,
    query_proj,
    key_proj,
    value_proj,
    output_proj,
    ffn_gain,
    router_proj,
    expert_gate,
    expert_up,
    expert_down,
):
    gain_attn, query_full, key_full, value_full, output_full = (
        lax.all_gather(attn_gain, "dp", axis=0, tiled=True),
        lax.all_gather(query_proj, "dp", axis=0, tiled=True),
        lax.all_gather(key_proj, "dp", axis=0, tiled=True),
        lax.all_gather(value_proj, "dp", axis=0, tiled=True),
        lax.all_gather(output_proj, "dp", axis=0, tiled=True),
    )
    inputs_f32 = tokens_in.astype(jnp.float32)
    gain_attn_f32 = gain_attn.astype(jnp.float32)
    normed_attn, inverse_attn = norm_forward(inputs_f32, gain_attn_f32)
    normed_all = lax.all_gather(normed_attn.astype(jnp.bfloat16), "tensor", axis=0, tiled=True)
    length = normed_all.shape[0]
    heads_local = query_full.shape[1] // HD
    kv_local = key_full.shape[1] // HD
    cosine, sine_table = rope_tables(length, HD)
    query_lin = jnp.dot(normed_all, query_full, preferred_element_type=jnp.float32).reshape(
        length, heads_local, HD
    )
    key_lin = jnp.dot(normed_all, key_full, preferred_element_type=jnp.float32).reshape(
        length, kv_local, HD
    )
    value_low = (
        jnp.dot(normed_all, value_full, preferred_element_type=jnp.float32)
        .astype(jnp.bfloat16)
        .reshape(length, kv_local, HD)
    )
    query_low = rotate(query_lin, cosine, sine_table).astype(jnp.bfloat16)
    key_low = rotate(key_lin, cosine, sine_table).astype(jnp.bfloat16)
    attended, log_total = attend(query_low, key_low, value_low)
    branch = lax.psum_scatter(
        jnp.einsum("sh,dh->sd", attended, output_full, preferred_element_type=jnp.float32).astype(
            jnp.bfloat16
        ),
        "tensor",
        scatter_dimension=0,
        tiled=True,
    ).astype(jnp.float32)
    residual = inputs_f32 + branch
    gain_ffn, router_full, gate_full, up_full, down_full = (
        lax.all_gather(ffn_gain, "dp", axis=0, tiled=True),
        lax.all_gather(router_proj, "dp", axis=0, tiled=True),
        lax.all_gather(expert_gate, "dp", axis=0, tiled=True),
        lax.all_gather(expert_up, "dp", axis=0, tiled=True),
        lax.all_gather(expert_down, "dp", axis=0, tiled=True),
    )
    gain_ffn_f32 = gain_ffn.astype(jnp.float32)
    normed_ffn, inverse_ffn = norm_forward(residual, gain_ffn_f32)
    ffn_all = lax.all_gather(normed_ffn.astype(jnp.bfloat16), "tensor", axis=0, tiled=True)
    model_width = ffn_all.shape[1]
    logits = jnp.dot(ffn_all, router_full, preferred_element_type=jnp.float32)
    gate_probs = jax.nn.softmax(jnp.take_along_axis(logits, routes, axis=1), axis=1)
    flat_routes = routes.reshape(-1)
    chosen = (flat_routes[:, None] == jnp.arange(E)[None, :]).astype(jnp.int32)
    position = jnp.sum((jnp.cumsum(chosen, axis=0) - 1) * chosen, axis=1)
    slot_index = flat_routes * CAP + position
    slot_owner = (
        jnp.zeros((E * CAP,), jnp.int32)
        .at[slot_index]
        .set(jnp.arange(flat_routes.shape[0], dtype=jnp.int32) // TOP)
    )
    slot_gate = jnp.zeros((E * CAP,), jnp.float32).at[slot_index].set(gate_probs.reshape(-1))
    packed = jnp.take(ffn_all, slot_owner, axis=0).reshape(E, CAP, model_width)
    gate_in = jnp.einsum("ecd,def->ecf", packed, gate_full, preferred_element_type=jnp.float32)
    up_in = jnp.einsum("ecd,def->ecf", packed, up_full, preferred_element_type=jnp.float32)
    sigmoid_gate = jax.nn.sigmoid(gate_in)
    activated = gate_in * sigmoid_gate
    hidden = (activated * up_in).astype(jnp.bfloat16)
    expert_out = jnp.einsum(
        "ecf,def->ecd", hidden, down_full, preferred_element_type=jnp.float32
    ).reshape(E * CAP, model_width)
    route_rows = jnp.take(expert_out, slot_index, axis=0).reshape(length, TOP, model_width)
    mixture = jnp.sum(gate_probs[:, :, None] * route_rows, axis=1)
    layer_output = (
        residual
        + lax.psum_scatter(
            mixture.astype(jnp.bfloat16), "tensor", scatter_dimension=0, tiled=True
        ).astype(jnp.float32)
    ).astype(jnp.bfloat16)
    cot_all = lax.all_gather(cotangent, "tensor", axis=0, tiled=True)
    grad_gates = jnp.sum(route_rows * cot_all[:, None, :], axis=2)
    grad_picked = gate_probs * (
        grad_gates - jnp.sum(gate_probs * grad_gates, axis=1, keepdims=True)
    )
    route_table = (routes[:, :, None] == jnp.arange(E)[None, None, :]).astype(jnp.float32)
    grad_logits = jnp.sum(grad_picked[:, :, None] * route_table, axis=1)
    grad_expert = (
        (slot_gate[:, None] * jnp.take(cot_all, slot_owner, axis=0))
        .astype(jnp.bfloat16)
        .reshape(E, CAP, model_width)
    )
    grad_hidden = jnp.einsum(
        "ecd,def->ecf", grad_expert, down_full, preferred_element_type=jnp.float32
    )
    grad_gate_in = (
        grad_hidden * up_in * sigmoid_gate * (1.0 + gate_in * (1.0 - sigmoid_gate))
    ).astype(jnp.bfloat16)
    grad_up_in = (grad_hidden * activated).astype(jnp.bfloat16)
    grad_gate_w = jnp.einsum(
        "ecd,ecf->def", packed, grad_gate_in, preferred_element_type=jnp.float32
    )
    grad_up_w = jnp.einsum("ecd,ecf->def", packed, grad_up_in, preferred_element_type=jnp.float32)
    grad_down_w = jnp.einsum(
        "ecd,ecf->def", grad_expert, hidden, preferred_element_type=jnp.float32
    )
    grad_experts = (
        lax.psum_scatter(grad_gate_w, "dp", scatter_dimension=0, tiled=True),
        lax.psum_scatter(grad_up_w, "dp", scatter_dimension=0, tiled=True),
        lax.psum_scatter(grad_down_w, "dp", scatter_dimension=0, tiled=True),
    )
    grad_packed = jnp.einsum(
        "ecf,def->ecd", grad_gate_in, gate_full, preferred_element_type=jnp.float32
    )
    grad_packed = grad_packed + jnp.einsum(
        "ecf,def->ecd", grad_up_in, up_full, preferred_element_type=jnp.float32
    )
    grad_packed = grad_packed.reshape(E * CAP, model_width)
    grad_ffn_all = jnp.sum(
        jnp.take(grad_packed, slot_index, axis=0).reshape(length, TOP, model_width), axis=1
    )
    router_f32 = router_full.astype(jnp.float32)
    grad_ffn_all = grad_ffn_all + jnp.einsum(
        "se,de->sd", grad_logits, router_f32, precision=HIGHEST_MODE
    )
    grad_router_part = jnp.einsum(
        "sd,se->de", ffn_all.astype(jnp.float32), grad_logits, precision=HIGHEST_MODE
    )
    grad_ffn_local = lax.psum_scatter(
        grad_ffn_all.astype(jnp.bfloat16), "tensor", scatter_dimension=0, tiled=True
    ).astype(jnp.float32)
    grad_resid_norm, grad_gain_ffn = norm_backward(
        residual, inverse_ffn, gain_ffn_f32, grad_ffn_local
    )
    grad_residual = cotangent.astype(jnp.float32) + grad_resid_norm
    branch_all = lax.all_gather(grad_residual.astype(jnp.bfloat16), "tensor", axis=0, tiled=True)
    grad_out_w = jnp.einsum("sd,sh->dh", branch_all, attended, preferred_element_type=jnp.float32)
    grad_attended = jnp.einsum(
        "sd,dh->sh", branch_all, output_full, preferred_element_type=jnp.float32
    ).astype(jnp.bfloat16)
    grad_queries, grad_keys, grad_values = attend_back(
        query_low, key_low, value_low, log_total, grad_attended
    )
    grad_query_lin = (
        unrotate(grad_queries, cosine, sine_table).astype(jnp.bfloat16).reshape(length, -1)
    )
    grad_key_lin = unrotate(grad_keys, cosine, sine_table).astype(jnp.bfloat16).reshape(length, -1)
    grad_value_low = grad_values.astype(jnp.bfloat16).reshape(length, -1)
    grad_query_w = jnp.einsum(
        "sd,sh->dh", normed_all, grad_query_lin, preferred_element_type=jnp.float32
    )
    grad_key_w = jnp.einsum(
        "sd,sh->dh", normed_all, grad_key_lin, preferred_element_type=jnp.float32
    )
    grad_value_w = jnp.einsum(
        "sd,sh->dh", normed_all, grad_value_low, preferred_element_type=jnp.float32
    )
    grad_attn_all = jnp.einsum(
        "sh,dh->sd", grad_query_lin, query_full, preferred_element_type=jnp.float32
    )
    grad_attn_all = grad_attn_all + jnp.einsum(
        "sh,dh->sd", grad_key_lin, key_full, preferred_element_type=jnp.float32
    )
    grad_attn_all = grad_attn_all + jnp.einsum(
        "sh,dh->sd", grad_value_low, value_full, preferred_element_type=jnp.float32
    )
    grad_attn_local = lax.psum_scatter(
        grad_attn_all.astype(jnp.bfloat16), "tensor", scatter_dimension=0, tiled=True
    ).astype(jnp.float32)
    grad_input_norm, grad_gain_attn = norm_backward(
        inputs_f32, inverse_attn, gain_attn_f32, grad_attn_local
    )
    grad_input = (grad_residual + grad_input_norm).astype(jnp.bfloat16)
    grad_attn = (
        lax.psum_scatter(grad_query_w, "dp", scatter_dimension=0, tiled=True),
        lax.psum_scatter(grad_key_w, "dp", scatter_dimension=0, tiled=True),
        lax.psum_scatter(grad_value_w, "dp", scatter_dimension=0, tiled=True),
        lax.psum_scatter(grad_out_w, "dp", scatter_dimension=0, tiled=True),
    )
    small_sums = (
        lax.psum_scatter(grad_gain_attn, ("dp", "tensor"), scatter_dimension=0, tiled=True),
        lax.psum_scatter(grad_gain_ffn, ("dp", "tensor"), scatter_dimension=0, tiled=True),
        lax.psum_scatter(grad_router_part, ("dp", "tensor"), scatter_dimension=0, tiled=True),
    )
    return (
        layer_output,
        grad_input,
        small_sums[0],
        grad_attn[0],
        grad_attn[1],
        grad_attn[2],
        grad_attn[3],
        small_sums[1],
        small_sums[2],
        grad_experts[0],
        grad_experts[1],
        grad_experts[2],
    )


def solution(mesh):
    return jax.shard_map(
        shards,
        mesh=mesh,
        in_specs=(
            P(("dp", "tensor"), None),
            P("dp", None),
            P(("dp", "tensor"), None),
            P("dp"),
            P("dp", "tensor"),
            P("dp", "tensor"),
            P("dp", "tensor"),
            P("dp", "tensor"),
            P("dp"),
            P("dp", None),
            P("dp", None, "tensor"),
            P("dp", None, "tensor"),
            P("dp", None, "tensor"),
        ),
        out_specs=(
            P(("dp", "tensor"), None),
            P(("dp", "tensor"), None),
            P(("dp", "tensor")),
            P("dp", "tensor"),
            P("dp", "tensor"),
            P("dp", "tensor"),
            P("dp", "tensor"),
            P(("dp", "tensor")),
            P(("dp", "tensor"), None),
            P("dp", None, "tensor"),
            P("dp", None, "tensor"),
            P("dp", None, "tensor"),
        ),
        check_vma=False,
    )
```

profile of v0, /device:TPU:0, one launch (start us, length us, event | category | flops | bytes accessed | tf_op | source)
XLA Modules:
  0.0 2343.9 jit_solution(14716738556937890734)
XLA Ops:
  10.9 173.0 %all-reduce.8 = (bf16[1536]{0:T(1024)(128)(2,1)S(1)}, bf16[1536]{0:T(1024)(128)(2,1)S(1)}) all-reduce(bf16[1536]{0:T(1024)(128)(2,1)S(1)} %dynamic-update-slice, bf16[1536]{0:T(1024)(128)(2,1)S(1)} %dynamic-update-slice.1), channel_id=1, replica_groups=mesh['dp'=64,'tensor'=2] {'dp'}, use_global_device_ids=true, to_apply=%add | all-reduce | flops 3072 | bytes 12288
  191.0 89.9 %all_gather.45 = bf16[1536,128]{1,0:T(8,128)(2,1)S(1)} all-gather(bf16[24,128]{1,0:T(8,128)(2,1)S(1)} %copy-done.68), channel_id=1, replica_groups=mesh['dp'=64,'tensor'=2] {'dp'}, dimensions={0}, use_global_device_ids=true | all-gather | bytes 399360 | tf_op jit(solution)/shard_map/all_gather | solution.py:144
  280.9 91.0 %all_gather.44 = bf16[1536,128]{1,0:T(8,128)(2,1)S(1)} all-gather(bf16[24,128]{1,0:T(8,128)(2,1)S(1)} %copy-done.69), channel_id=1, replica_groups=mesh['dp'=64,'tensor'=2] {'dp'}, dimensions={0}, use_global_device_ids=true | all-gather | bytes 399360 | tf_op jit(solution)/shard_map/all_gather | solution.py:145
  403.9 22.4 reduce-scatter.17.cloned.1.call-done
  436.7 96.2 %all-gather = bf16[64,24,8]{1,2,0:T(8,128)(2,1)S(1)} all-gather(bf16[1,24,8]{1,2,0:T(8,128)(2,1)S(1)} %bitcast.216), channel_id=1, replica_groups=mesh['dp'=64,'tensor'=2] {'dp'}, dimensions={0}, use_global_device_ids=true | all-gather | bytes 24960 | tf_op jit(solution)/shard_map/all_gather | solution.py:181
  534.2 8.4 scatter_custom_fusion
  543.9 7.1 mul.412
  551.0 15.3 mul.413
  566.3 9.6 gather_fusion.3
  577.8 12.5 gather_fusion
  590.7 9.6 gather_fusion.1
  600.3 7.3 broadcast_select_fusion
  607.6 12.1 fusion.86
  619.7 48.0 %all-gather.21.cloned.1.call-done = bf16[1536,8,384]{2,0,1:T(8,128)(2,1)} async-done(((bf16[24,8,384]{2,0,1:T(8,128)(2,1)}), bf16[1536,8,384]{2,0,1:T(8,128)(2,1)}) %all-gather.21.cloned.1.call-update) | async-done | bytes 9437200 | tf_op jit(solution)/shard_map/all_gather | solution.py:183
  667.6 13.3 multiply_convert_fusion.3
  680.9 72.8 %all-gather.23.cloned.1.call-done = bf16[1536,8,384]{2,0,1:T(8,128)(2,1)} async-done(((bf16[24,8,384]{2,0,1:T(8,128)(2,1)}), bf16[1536,8,384]{2,0,1:T(8,128)(2,1)}) %all-gather.23.cloned.1.call-update) | async-done | bytes 9437200 | tf_op jit(solution)/shard_map/all_gather | solution.py:184
  753.7 13.3 fusion.87
  767.0 19.9 gather_fusion.2
  786.9 13.3 multiply_reduce_fusion
  800.9 8.2 scatter_custom_fusion.1
  809.1 5.1 multiply_convert_fusion
  814.2 13.9 multiply_convert_fusion.1
  828.1 14.0 fusion.88
  842.2 15.8 convolution_add_fusion
  858.0 19.7 gather_fusion.4
  877.7 9.9 broadcast_select_fusion.1
  887.6 14.7 reshape.441
  902.3 13.0 reduce_sum.148
  915.4 4.7 fusion.13
  920.1 26.4 %reduce-scatter.21.cloned.1.call-done = bf16[256,1536]{1,0:T(8,128)(2,1)} async-done(((bf16[512,1536]{1,0:T(8,128)(2,1)}), bf16[256,1536]{1,0:T(8,128)(2,1)}) %reduce-scatter.21.cloned.1.call-update) | async-done | bytes 786448 | tf_op jit(solution)/shard_map/reduce_scatter | solution.py:267
  951.1 30.8 %all-gather.27.cloned.1.call-done = bf16[512,1536]{1,0:T(8,128)(2,1)} async-done(((bf16[256,1536]{1,0:T(8,128)(2,1)}), bf16[512,1536]{1,0:T(8,128)(2,1)}) %all-gather.27.cloned.1.call-update) | async-done | bytes 1572880 | tf_op jit(solution)/shard_map/all_gather | solution.py:274
  1006.6 14.8 reshape.438
  1021.4 12.5 multiply_reduce_fusion.1
  1037.2 5.3 fusion.92
  1042.5 4.7 fusion.90
  1047.3 12.5 convolution_bitcast_fusion
  1059.9 18.9 copy.165
  1079.0 12.2 convolution_bitcast_fusion.2
  1091.3 19.0 copy.163
  1110.4 12.1 convolution_bitcast_fusion.1
  1122.5 19.0 copy.164
  1145.2 66.9 %all-reduce.7 = (f32[1536]{0:T(1024)S(1)}, f32[1536]{0:T(1024)S(1)}, f32[1536,8]{0,1:T(8,128)S(1)}) all-reduce(f32[1536]{0:T(1024)S(1)} %get-tuple-element.85, f32[1536]{0:T(1024)S(1)} %copy-done.56, f32[1536,8]{0,1:T(8,128)S(1)} %fusion.93), channel_id=6, replica_groups=mesh['dp'=64,'tensor'=2] {'dp','tensor'}, use_global_device_ids=true, to_apply=%region_24.27.clone | all-reduce | flops 15360 | bytes 122880
  1218.2 145.3 %reduce-scatter.35.cloned.1.call-done = f32[24,128]{1,0:T(8,128)} async-done(((f32[1536,128]{1,0:T(8,128)}), f32[24,128]{1,0:T(8,128)}) %reduce-scatter.35.cloned.1.call-update) | async-done | bytes 12304
  1363.6 155.2 %reduce-scatter.27.cloned.1.call-done = f32[24,768]{1,0:T(8,128)} async-done(((f32[1536,768]{1,0:T(8,128)}), f32[24,768]{1,0:T(8,128)}) %reduce-scatter.27.cloned.1.call-update) | async-done | bytes 73744 | tf_op jit(solution)/shard_map/reduce_scatter | solution.py:316
  1518.8 155.2 %reduce-scatter.25.cloned.1.call-done = f32[24,768]{1,0:T(8,128)} async-done(((f32[1536,768]{1,0:T(8,128)}), f32[24,768]{1,0:T(8,128)}) %reduce-scatter.25.cloned.1.call-update) | async-done | bytes 73744 | tf_op jit(solution)/shard_map/reduce_scatter | solution.py:313
  1674.0 220.7 %reduce-scatter.33.cloned.1.call-done = f32[24,8,384]{2,1,0:T(8,128)} async-done(((f32[1536,8,384]{2,1,0:T(8,128)}), f32[24,8,384]{2,1,0:T(8,128)}) %reduce-scatter.33.cloned.1.call-update) | async-done | bytes 294928 | tf_op jit(solution)/shard_map/reduce_scatter | solution.py:248
  1894.7 221.6 %reduce-scatter.29.cloned.1.call-done = f32[24,8,384]{2,1,0:T(8,128)} async-done(((f32[1536,8,384]{2,1,0:T(8,128)}), f32[24,8,384]{2,1,0:T(8,128)}) %reduce-scatter.29.cloned.1.call-update) | async-done | bytes 294928 | tf_op jit(solution)/shard_map/reduce_scatter | solution.py:246
  2116.3 220.5 %reduce-scatter.31.cloned.1.call-done = f32[24,8,384]{2,1,0:T(8,128)} async-done(((f32[1536,8,384]{2,1,0:T(8,128)}), f32[24,8,384]{2,1,0:T(8,128)}) %reduce-scatter.31.cloned.1.call-update) | async-done | bytes 294928 | tf_op jit(solution)/shard_map/reduce_scatter | solution.py:247
  (300 shorter events, 100.0 us)
Async XLA Ops:
  7.2 183.8 %copy-start.68 = (bf16[24,128]{1,0:T(8,128)(2,1)S(1)}, bf16[24,128]{1,0:T(8,128)(2,1)}, u32[]{:S(2)}) copy-start(bf16[24,128]{1,0:T(8,128)(2,1)} %param.22) | copy-start | bytes 18436
  7.2 273.7 %copy-start.69 = (bf16[24,128]{1,0:T(8,128)(2,1)S(1)}, bf16[24,128]{1,0:T(8,128)(2,1)}, u32[]{:S(2)}) copy-start(bf16[24,128]{1,0:T(8,128)(2,1)} %param.23) | copy-start | bytes 18436
  7.2 365.5 %all-gather.11.cloned.1.call-start = ((), (), s32[]{:S(2)}) async-start(), calls=%async_computation.11 | async-start | bytes 2359296 | tf_op jit(solution)/shard_map/all_gather | solution.py:151
  188.6 191.6 %all-gather.13.cloned.1.call-start = ((), (), s32[]{:S(2)}) async-start(), calls=%async_computation.12 | async-start | bytes 2396160 | tf_op jit(solution)/shard_map/all_gather | solution.py:143
  189.4 208.7 %all-gather.15.cloned.1.call-start = ((), (), s32[]{:S(2)}) async-start(), calls=%async_computation.13 | async-start | bytes 2396160 | tf_op jit(solution)/shard_map/all_gather | solution.py:146
  190.1 236.2 %reduce-scatter.17.cloned.1.call-start = ((), (), s32[]{:S(2)}) async-start(), calls=%async_computation.14 | async-start | bytes 2359296 | tf_op jit(solution)/shard_map/reduce_scatter | solution.py:170
  280.9 95.6 %copy-start.24 = (bf16[1536,128]{1,0:T(8,128)(2,1)}, bf16[1536,128]{1,0:T(8,128)(2,1)S(1)}, u32[]{:S(2)}) copy-start(bf16[1536,128]{1,0:T(8,128)(2,1)S(1)} %all_gather.45) | copy-start | bytes 1179652
  403.2 23.2 copy-start.4
  403.2 140.7 %all-gather.25.cloned.1.call-start = ((), (), s32[]{:S(2)}) async-start(), calls=%async_computation.20 | async-start | bytes 2359296 | tf_op jit(solution)/shard_map/all_gather | solution.py:219
  403.8 172.0 %all-gather.17.cloned.1.call-start = ((), (), s32[]{:S(2)}) async-start(), calls=%async_computation.15 | async-start | bytes 2359296 | tf_op jit(solution)/shard_map/all_gather | solution.py:188
  403.9 26.9 %copy-start.40 = (f32[1536]{0:T(1024)}, f32[1536]{0:T(1024)S(1)}, u32[]{:S(2)}) copy-start(f32[1536]{0:T(1024)S(1)} %convert_element_type.150) | copy-start | bytes 18436
  403.9 26.9 %copy-start.48 = (bf16[24,8,384]{2,1,0:T(8,128)(2,1)S(1)}, bf16[24,8,384]{2,1,0:T(8,128)(2,1)}, u32[]{:S(2)}) copy-start(bf16[24,8,384]{2,1,0:T(8,128)(2,1)} %param.27) | copy-start | bytes 442372
  403.9 27.7 %copy-start.49 = (bf16[24,8,384]{2,1,0:T(8,128)(2,1)S(1)}, bf16[24,8,384]{2,1,0:T(8,128)(2,1)}, u32[]{:S(2)}) copy-start(bf16[24,8,384]{2,1,0:T(8,128)(2,1)} %param.28) | copy-start | bytes 442372
  430.7 176.8 %all-gather.19.cloned.1.call-start = ((), (), s32[]{:S(2)}) async-start(), calls=%async_computation.16 | async-start | bytes 9584640 | tf_op jit(solution)/shard_map/all_gather | solution.py:182
  431.5 236.1 %all-gather.21.cloned.1.call-start = ((), (), s32[]{:S(2)}) async-start(), calls=%async_computation.17 | async-start | bytes 9584640 | tf_op jit(solution)/shard_map/all_gather | solution.py:183
  432.3 321.4 %all-gather.23.cloned.1.call-start = ((), (), s32[]{:S(2)}) async-start(), calls=%async_computation.18 | async-start | bytes 9584640 | tf_op jit(solution)/shard_map/all_gather | solution.py:184
  433.0 513.4 %reduce-scatter.21.cloned.1.call-start = ((), (), s32[]{:S(2)}) async-start(), calls=%async_computation.21 | async-start | bytes 2359296 | tf_op jit(solution)/shard_map/reduce_scatter | solution.py:267
  533.1 42.7 %copy-start.38 = (bf16[1536,8]{0,1:T(8,128)(2,1)}, bf16[1536,8]{0,1:T(8,128)(2,1)S(1)}, u32[]{:S(2)}) copy-start(bf16[1536,8]{0,1:T(8,128)(2,1)S(1)} %reshape.519) | copy-start | bytes 73732
  551.0 15.3 copy-start.2
  577.8 12.9 copy-start
  680.9 86.1 %copy-start.10 = (bf16[8,320,384]{2,1,0:T(8,128)(2,1)}, bf16[8,320,384]{2,1,0:T(8,128)(2,1)S(1)}, u32[]{:S(2)}) copy-start(bf16[8,320,384]{2,1,0:T(8,128)(2,1)S(1)} %get-tuple-element.121) | copy-start | bytes 5898244
  753.7 13.3 copy-start.53
  767.0 19.9 copy-start.60
  800.7 114.6 %copy-start.46 = (f32[512,8]{0,1:T(8,128)}, f32[512,8]{0,1:T(8,128)S(1)}, u32[]{:S(2)}) copy-start(f32[512,8]{0,1:T(8,128)S(1)} %select_reduce_fusion) | copy-start | bytes 49156
  814.2 14.0 copy-start.8
  828.1 14.0 copy-start.11
  902.3 13.0 copy-start.39
  915.4 31.1 %copy-start.5 = (bf16[256,1536]{1,0:T(8,128)(2,1)S(1)}, bf16[256,1536]{1,0:T(8,128)(2,1)}, u32[]{:S(2)}) copy-start(bf16[256,1536]{1,0:T(8,128)(2,1)} %param.17) | copy-start | bytes 2359300
  915.4 31.1 %copy-start.9 = (bf16[256,1536]{1,0:T(8,128)(2,1)S(1)}, bf16[256,1536]{1,0:T(8,128)(2,1)}, u32[]{:S(2)}) copy-start(bf16[256,1536]{1,0:T(8,128)(2,1)} %reduce-scatter.17.cloned.1.call-done) | copy-start | bytes 2359300
  915.4 31.1 %copy-start.41 = (f32[1536]{0:T(1024)S(1)}, f32[1536]{0:T(1024)}, u32[]{:S(2)}) copy-start(f32[1536]{0:T(1024)} %copy-done.40) | copy-start | bytes 18436
  915.4 31.1 %copy-start.58 = (f32[256]{0:T(256)S(1)}, f32[256]{0:T(256)}, u32[]{:S(2)}) copy-start(f32[256]{0:T(256)} %copy-done.57) | copy-start | bytes 3076
  920.0 29.4 %copy-start.16 = (bf16[256,1536]{1,0:T(8,128)(2,1)S(1)}, bf16[256,1536]{1,0:T(8,128)(2,1)}, u32[]{:S(2)}) copy-start(bf16[256,1536]{1,0:T(8,128)(2,1)} %param.19) | copy-start | bytes 2359300
  920.0 29.4 %copy-start.63 = (f32[256]{0:T(256)S(1)}, f32[256]{0:T(256)}, u32[]{:S(2)}) copy-start(f32[256]{0:T(256)} %get-tuple-element.115) | copy-start | bytes 3076
  920.1 61.8 %all-gather.27.cloned.1.call-start = ((), (), s32[]{:S(2)}) async-start(), calls=%async_computation.22 | async-start | bytes 2359296 | tf_op jit(solution)/shard_map/all_gather | solution.py:274
  951.0 192.6 %reduce-scatter.23.cloned.1.call-start = ((), (), s32[]{:S(2)}) async-start(), calls=%async_computation.23 | async-start | bytes 2359296 | tf_op jit(solution)/shard_map/reduce_scatter | solution.py:305
  1006.4 207.6 %reduce-scatter.19.cloned.1.call-start = ((), (), s32[]{:S(2)}) async-start(), calls=%async_computation.19 | async-start | bytes 2359296 | tf_op jit(solution)/shard_map/reduce_scatter | solution.py:215
  1034.0 184.3 %reduce-scatter.37.cloned.1.call-start = ((), (), s32[]{:S(2)}) async-start(), calls=%async_computation.30 | async-start | bytes 798720
  1035.6 328.0 %reduce-scatter.35.cloned.1.call-start = ((), (), s32[]{:S(2)}) async-start(), calls=%async_computation.29 | async-start | bytes 798720
  1037.2 481.6 %reduce-scatter.27.cloned.1.call-start = ((), (), s32[]{:S(2)}) async-start(), calls=%async_computation.25 | async-start | bytes 4792320 | tf_op jit(solution)/shard_map/reduce_scatter | solution.py:316
  1042.5 631.5 %reduce-scatter.25.cloned.1.call-start = ((), (), s32[]{:S(2)}) async-start(), calls=%async_computation.24 | async-start | bytes 4792320 | tf_op jit(solution)/shard_map/reduce_scatter | solution.py:313
  1047.3 847.4 %reduce-scatter.33.cloned.1.call-start = ((), (), s32[]{:S(2)}) async-start(), calls=%async_computation.28 | async-start | bytes 19169280 | tf_op jit(solution)/shard_map/reduce_scatter | solution.py:248
  1078.8 1037.5 %reduce-scatter.29.cloned.1.call-start = ((), (), s32[]{:S(2)}) async-start(), calls=%async_computation.26 | async-start | bytes 19169280 | tf_op jit(solution)/shard_map/reduce_scatter | solution.py:246
  1110.3 1226.5 %reduce-scatter.31.cloned.1.call-start = ((), (), s32[]{:S(2)}) async-start(), calls=%async_computation.27 | async-start | bytes 19169280 | tf_op jit(solution)/shard_map/reduce_scatter | solution.py:247
  1141.5 72.5 %copy-start.42 = (f32[1536]{0:T(1024)S(1)}, f32[1536]{0:T(1024)}, u32[]{:S(2)}) copy-start(f32[1536]{0:T(1024)} %copy-done.40) | copy-start | bytes 18436
  1141.5 72.5 %copy-start.59 = (f32[256]{0:T(256)S(1)}, f32[256]{0:T(256)}, u32[]{:S(2)}) copy-start(f32[256]{0:T(256)} %copy-done.57) | copy-start | bytes 3076
  1141.5 72.5 %copy-start.64 = (f32[256]{0:T(256)S(1)}, f32[256]{0:T(256)}, u32[]{:S(2)}) copy-start(f32[256]{0:T(256)} %get-tuple-element.115) | copy-start | bytes 3076
  1141.5 72.5 %copy-start.66 = (f32[256]{0:T(256)S(1)}, f32[256]{0:T(256)}, u32[]{:S(2)}) copy-start(f32[256]{0:T(256)} %copy-done.65) | copy-start | bytes 3076
  1141.5 72.5 %copy-start.70 = (f32[256]{0:T(256)S(1)}, f32[256]{0:T(256)}, u32[]{:S(2)}) copy-start(f32[256]{0:T(256)} %get-tuple-element.113) | copy-start | bytes 3076
  (47 other events, 132.2 us)
Sparse Core Ops, SparseCore 0:
  188.7 24.0 all-gather.10
  216.1 69.3 all-gather.12
  288.8 65.1 all-gather.14
  403.3 22.9 reduce-scatter.16
  428.0 30.7 all-gather.24
  460.9 30.6 all-gather.16
  495.9 85.6 all-gather.18
  585.3 82.2 all-gather.20
  671.4 82.2 all-gather.22
  920.2 26.2 reduce-scatter.20
  951.1 30.7 all-gather.26
  1006.5 29.5 reduce-scatter.22
  1038.6 29.5 reduce-scatter.18
  1073.7 144.1 reduce-scatter.36
  1223.3 140.1 reduce-scatter.34
  1369.4 149.3 reduce-scatter.26
  1524.6 149.3 reduce-scatter.24
  1680.5 214.1 reduce-scatter.32
  1902.5 213.7 reduce-scatter.28
  2122.8 213.8 reduce-scatter.30
where the time goes:
time: 2360 us; the launch traced here: 2340 us
  waiting for transfers between devices  1320 us (56%)
  blocking collectives  517 us (22%)
  local copies, waits for them, and re-layouts  223 us (9%)
  matrix products  171 us (7%)
  other arithmetic  94.2 us (4%)
    unnamed x2, blocking collectives  240 us
    reduce_scatter x1, waiting for transfers between devices, shards(): lax.psum_scatter(grad_gate_w, 'dp', scatter_dimension=0, tiled=True)  222 us
    reduce_scatter x1, waiting for transfers between devices, shards(): lax.psum_scatter(grad_down_w, 'dp', scatter_dimension=0, tiled=True)  221 us
    reduce_scatter x1, waiting for transfers between devices, shards(): lax.psum_scatter(grad_up_w, 'dp', scatter_dimension=0, tiled=True)  220 us
    reduce_scatter x1, waiting for transfers between devices, shards(): lax.psum_scatter(grad_query_w, 'dp', scatter_dimension=0, tiled=True)  155 us
    reduce_scatter x1, waiting for transfers between devices, shards(): lax.psum_scatter(grad_out_w, 'dp', scatter_dimension=0, tiled=True)  155 us
    unnamed x22, waiting for transfers between devices  148 us
    all_gather x1, blocking collectives, shards(): lax.all_gather(router_proj, 'dp', axis=0, tiled=True)  96.2 us
  transfers between devices with their start and end apart: 20, of which 11 were waited for; matrix products, arithmetic and copies ran while one was open for 12% of the time, Pallas kernels for 0%

commit v1 on v0

v1 whole, which is shorter than its diff:
```python
import functools

import jax
import jax.numpy as jnp
from jax import lax
from jax.experimental import pallas as pl
from jax.experimental.pallas import tpu as pltpu
from jax.sharding import PartitionSpec as P

HD = 128
E = 8
D = 1536
SEQ = 512
OWN = 256
HALF = 768
QKV = 1024
ATT = 1792
WIDE = 1920
NORM_EPSILON = 1e-06
ROPE_BASE = 1000000.0
MESH = pl.DeviceIdType.MESH
BF = jnp.bfloat16
F32 = jnp.float32
ANY = pl.BlockSpec(memory_space=pl.ANY)
VMEM = pl.BlockSpec(memory_space=pltpu.VMEM)
MIB = 1 << 20


def place():
    d = lax.axis_index("dp")
    t = lax.axis_index("tensor")
    c = lax.rem(d, 2)
    z = lax.rem(lax.div(d, 2), 4)
    x = lax.rem(lax.div(d, 8), 4)
    yh = lax.div(d, 32)
    return yh, x, z, c, t


def device(yh, x, z, c, t):
    return (((yh * 4 + x) * 4 + z) * 2 + c, t)


def up4(v, k):
    return lax.rem(v + k, 4)


def up2(v, k):
    return lax.rem(v + k, 2)


class Links:
    def __init__(self, send_sems, local_sems):
        self.me = place()
        self.send_sems, self.local_sems = send_sems, local_sems
        self.sent, self.local = [], []

    def at(self, dy=0, dx=0, dz=0, dc=0):
        yh, x, z, c, t = self.me
        y = up4(yh * 2 + t, dy)
        return device(lax.div(y, 2), up4(x, dx), up4(z, dz), up2(c, dc), lax.rem(y, 2))

    def flip(self, dyh=0, dt=0, dc=0):
        yh, x, z, c, t = self.me
        return device(up2(yh, dyh), x, z, up2(c, dc), up2(t, dt))

    def barrier(self, partners):
        sem = pltpu.get_barrier_semaphore()
        for partner in partners:
            pl.semaphore_signal(sem, inc=1, device_id=partner, device_id_type=MESH)
        pl.semaphore_wait(sem, len(partners))

    def send(self, src, dst, recv_sem, target):
        copy = pltpu.make_async_remote_copy(
            src_ref=src,
            dst_ref=dst,
            send_sem=self.send_sems.at[len(self.sent)],
            recv_sem=recv_sem,
            device_id=target,
            device_id_type=MESH,
        )
        copy.start()
        self.sent.append(copy)
        return copy

    def keep(self, src, dst):
        copy = pltpu.make_async_copy(src, dst, self.local_sems.at[len(self.local)])
        copy.start()
        self.local.append(copy)
        return copy

    def finish(self):
        for copy in self.sent:
            copy.wait_send()


ALONG = [dict(dx=k) for k in (1, 2, 3)] + [dict(dz=k) for k in (1, 2, 3)]
RING = [dict(dy=k) for k in (1, 2, 3)]


def plane_gather(links, block, own_block, sems, arrived):
    _, x, z, _, _ = links.me
    pending = {}

    def hop(h, da, db, src, dst, k, second):
        along_x = (h == 0) != second
        target = links.at(dx=k) if along_x else links.at(dz=k)
        key = (h, da, (4 - k) % 4) if second else (h, (4 - k) % 4, 0)
        pending[key] = links.send(src, dst, sems.at[(key[0] * 4 + key[1]) * 4 + key[2]], target)

    def spot(h, da, db):
        return block(h, up4(x, da), up4(z, db)) if h == 0 else block(h, up4(x, db), up4(z, da))

    for k in (1, 3, 2):
        for h in (0, 1):
            hop(h, 0, 0, own_block(h), spot(h, 0, 0), k, False)
    for k in (1, 3, 2):
        for h in (0, 1):
            hop(h, 0, 0, own_block(h), spot(h, 0, 0), k, True)
    for da in (1, 3, 2):
        for h in (0, 1):
            pending[(h, da, 0)].wait_recv()
            for k in (1, 3, 2):
                hop(h, da, 0, spot(h, da, 0), spot(h, da, 0), k, True)
            arrived(h, spot(h, da, 0), da, 0)
    for da in (0, 1, 3, 2):
        for db in (1, 3, 2):
            for h in (0, 1):
                pending[(h, da, db)].wait_recv()
                arrived(h, spot(h, da, db), da, db)


def gather_attention_kernel(
    a, e, tok, cot, a_all, e_mine, tok_pair, cot_all,
    send_sems, local_sems, ring_sems, plane_sems, twin_sems, expert_sems, token_sems, cot_sems, cot_twin_sems,
):
    links = Links(send_sems, local_sems)
    yh, x, z, c, t = links.me
    y = yh * 2 + t
    cross = [dict(dy=k, dc=1) for k in (1, 2, 3)]
    links.barrier([links.at(**w) for w in ALONG + RING + cross + [dict(dc=1)]])

    ring = {}
    here = a_all.at[t, yh, x, z, c]
    for k in (1, 3, 2):
        ring[(4 - k) % 4] = links.send(a, here, ring_sems.at[(4 - k) % 4], links.at(dy=k))
    kept = [links.keep(a, here)]

    experts = []
    columns = pl.ds(pl.multiple_of(t * 384, 384), 384)
    slot = e_mine.at[:, yh, c, :, columns]
    for dy in range(4):
        for dc in range(2):
            src = e.at[up4(y, dy) * 2 + up2(c, dc)]
            if dy == 0 and dc == 0:
                kept.append(links.keep(src, slot))
            else:
                index = ((4 - dy) % 4) * 2 + dc
                experts.append(links.send(src, slot, expert_sems.at[index], links.at(dy=dy, dc=dc)))
    partner = links.flip(dt=1)
    kept.append(links.keep(tok, tok_pair.at[t]))
    token = links.send(tok, tok_pair.at[t], token_sems.at[0], partner)
    cots = {}
    for k in (1, 3, 2):
        cots[(4 - k) % 4] = links.send(cot, cot_all.at[y, c], cot_sems.at[(4 - k) % 4], links.at(dy=k))
    kept.append(links.keep(cot, cot_all.at[y, c]))
    twin = links.at(dc=1)
    twins = [links.send(cot, cot_all.at[y, c], cot_twin_sems.at[0], twin)]

    for copy in kept[:1]:
        copy.wait()
    for k in (1, 3, 2):
        ring[k].wait_recv()
    twins.append(links.send(a_all.at[:, :, x, z, c], a_all.at[:, :, x, z, c], twin_sems.at[0], twin))

    def arrived(h, ref, da, db):
        twins.append(links.send(ref, ref, twin_sems.at[(h * 4 + da) * 4 + db + 1], twin))

    def block(h, xo, zo):
        return a_all.at[h, :, xo, zo, c]

    plane_gather(links, block, lambda h: block(h, x, z), plane_sems, arrived)
    for k in (1, 3, 2):
        cots[k].wait_recv()
        ref = cot_all.at[up4(y, k), c]
        twins.append(links.send(ref, ref, cot_twin_sems.at[k], twin))
    token.wait_recv()
    for copy in experts:
        copy.wait_recv()
    for copy in twins:
        copy.wait_recv()
    for copy in kept[1:]:
        copy.wait()
    links.finish()


def gather_attention(a, e, tok, cot):
    return pl.pallas_call(
        gather_attention_kernel,
        out_shape=(
            jax.ShapeDtypeStruct((2, 2, 4, 4, 2, 24, WIDE), BF),
            jax.ShapeDtypeStruct((3, 2, 2, 24, 768), BF),
            jax.ShapeDtypeStruct((2, OWN, D), BF),
            jax.ShapeDtypeStruct((4, 2, OWN, D), BF),
        ),
        in_specs=[ANY] * 4,
        out_specs=(ANY,) * 4,
        scratch_shapes=[pltpu.SemaphoreType.DMA((n,)) for n in (96, 8, 4, 32, 33, 8, 1, 4, 4)],
        compiler_params=pltpu.CompilerParams(collective_id=1, has_side_effects=True),
        name="gather_attention",
    )(a, e, tok, cot)


def gather_experts_kernel(
    e_mine, tok, gates, e_all, tok_all, gates_all,
    send_sems, local_sems, plane_sems, token_sems, token_twin_sems, gate_sems, gate_twin_sems,
):
    links = Links(send_sems, local_sems)
    yh, x, z, c, t = links.me
    y = yh * 2 + t
    links.barrier([links.at(**w) for w in ALONG + RING + [dict(dc=1)]])
    twin = links.at(dc=1)
    tokens, gate = {}, {}
    for k in (1, 3, 2):
        j = (4 - k) % 4
        gate[j] = links.send(gates, gates_all.at[y, c], gate_sems.at[j], links.at(dy=k))
        tokens[j] = links.send(tok, tok_all.at[y, c], token_sems.at[j], links.at(dy=k))
    twins = [
        links.send(gates, gates_all.at[y, c], gate_twin_sems.at[0], twin),
        links.send(tok, tok_all.at[y, c], token_twin_sems.at[0], twin),
    ]
    kept = [links.keep(tok, tok_all.at[y, c]), links.keep(gates, gates_all.at[y, c])]
    kept.append(links.keep(e_mine, e_all.at[:, :, x, z]))

    def block(h, xo, zo):
        return e_all.at[:, h, xo, zo]

    plane_gather(links, block, lambda h: e_mine.at[:, h], plane_sems, lambda h, ref, da, db: None)
    for k in (1, 3, 2):
        gate[k].wait_recv()
        ref = gates_all.at[up4(y, k), c]
        twins.append(links.send(ref, ref, gate_twin_sems.at[k], twin))
        tokens[k].wait_recv()
        ref = tok_all.at[up4(y, k), c]
        twins.append(links.send(ref, ref, token_twin_sems.at[k], twin))
    for copy in twins:
        copy.wait_recv()
    for copy in kept:
        copy.wait()
    links.finish()


def gather_experts(e_mine, tok, gates):
    return pl.pallas_call(
        gather_experts_kernel,
        out_shape=(
            jax.ShapeDtypeStruct((3, 2, 4, 4, 2, 24, 768), BF),
            jax.ShapeDtypeStruct((4, 2, OWN, D), BF),
            jax.ShapeDtypeStruct((4, 2, 8, OWN), F32),
        ),
        in_specs=[ANY] * 3,
        out_specs=(ANY,) * 3,
        scratch_shapes=[pltpu.SemaphoreType.DMA((n,)) for n in (48, 4, 32, 4, 4, 4, 4)],
        compiler_params=pltpu.CompilerParams(collective_id=2, has_side_effects=True),
        name="gather_experts",
    )(e_mine, tok, gates)


class TokenSum:
    SCRATCH = [
        pltpu.VMEM((4, OWN, D), BF),
        pltpu.VMEM((4, OWN, D), BF),
        pltpu.VMEM((3, OWN, D), BF),
        pltpu.SemaphoreType.DMA((4,)),
        pltpu.SemaphoreType.DMA((4,)),
    ]

    def __init__(self, links, src, own, twin, ring, twin_sems, ring_sems):
        self.links, self.own, self.twin, self.ring, self.ring_sems = links, own, twin, ring, ring_sems
        yh, _, _, c, t = links.me
        y = yh * 2 + t
        self.order = (2, 1, 3, 0)
        self.twins, self.kept = {}, {}
        for k in self.order:
            self.twins[k] = links.send(src.at[up4(y, k), 1 - c], twin.at[k], twin_sems.at[k], links.at(dc=1))
            self.kept[k] = links.keep(src.at[up4(y, k), c], own.at[k])

    def spread(self):
        self.sent = {}
        for k in self.order:
            self.kept[k].wait()
            self.twins[k].wait_recv()

            def add(i, carry):
                rows = pl.ds(pl.multiple_of(i * 64, 64), 64)
                self.own[k, rows, :] = (self.own[k, rows, :].astype(F32) + self.twin[k, rows, :].astype(F32)).astype(BF)
                return carry

            lax.fori_loop(0, OWN // 64, add, 0)
            if k:
                j = (4 - k) % 4
                self.sent[j] = self.links.send(
                    self.own.at[k], self.ring.at[j - 1], self.ring_sems.at[j], self.links.at(dy=k)
                )

    def total(self, out):
        for j in (1, 3, 2):
            self.sent[j].wait_recv()

        def add(i, carry):
            rows = pl.ds(pl.multiple_of(i * 64, 64), 64)
            part = self.own[0, rows, :].astype(F32)
            for j in range(3):
                part = part + self.ring[j, rows, :].astype(F32)
            out[rows, :] = part
            return carry

        lax.fori_loop(0, OWN // 64, add, 0)


def add_blocks(refs, out, count):
    def body(i, carry):
        part = refs[0][i].astype(F32)
        for ref in refs[1:]:
            part = part + ref[i].astype(F32)
        out[i] = part.astype(out.dtype)
        return carry

    lax.fori_loop(0, count, body, 0)


def reduce_experts_kernel(
    g, gx, ge, gx_out,
    own, first, mid, second, last,
    tok_own, tok_twin, tok_ring, tok_twin_sems, tok_ring_sems,
    send_sems, local_sems, first_sems, second_sems, expert_sems,
):
    links = Links(send_sems, local_sems)
    yh, x, z, c, t = links.me
    y = yh * 2 + t
    cross = [dict(dy=k, dc=1) for k in (1, 2, 3)]
    links.barrier([links.at(**w) for w in ALONG + RING + cross + [dict(dc=1)]])
    tokens = TokenSum(links, gx, tok_own, tok_twin, tok_ring, tok_twin_sems, tok_ring_sems)

    arrive = {}
    for k in (2, 1, 3):
        j = (4 - k) % 4
        arrive[(0, j)] = links.send(
            g.at[:, 0, :, up4(z, k)], first.at[0, j - 1], first_sems.at[j - 1], links.at(dz=k)
        )
        arrive[(1, j)] = links.send(
            g.at[:, 1, up4(x, k)], first.at[1, j - 1], first_sems.at[3 + j - 1], links.at(dx=k)
        )
    kept = [links.keep(g.at[:, 0, :, z], own.at[0]), links.keep(g.at[:, 1, x], own.at[1])]
    tokens.spread()
    for copy in kept:
        copy.wait()
    for j in (1, 3, 2):
        for h in (0, 1):
            arrive[(h, j)].wait_recv()
    final = {}
    for k in (2, 1, 3, 0):
        for h in (0, 1):
            place_of = up4(x, k) if h == 0 else up4(z, k)

            def body(i, carry):
                part = own[h, i, place_of].astype(F32)
                for j in range(3):
                    part = part + first[h, j, i, place_of].astype(F32)
                mid[h, k, i] = part.astype(BF)
                return carry

            lax.fori_loop(0, 3, body, 0)
            if k:
                j = (4 - k) % 4
                target = links.at(dx=k) if h == 0 else links.at(dz=k)
                final[(h, j)] = links.send(
                    mid.at[h, k], second.at[h, j - 1], second_sems.at[h * 3 + j - 1], target
                )
    tokens.total(gx_out)
    for h in (0, 1):
        for j in (1, 3, 2):
            final[(h, j)].wait_recv()
        add_blocks([mid.at[h, 0], second.at[h, 0], second.at[h, 1], second.at[h, 2]], last.at[h], 3)
    back, slot = [], y * 2 + c
    for dyh in range(2):
        for dt in range(2):
            for dc in range(2):
                columns = pl.ds(pl.multiple_of(up2(t, dt) * 384, 384), 384)
                src = last.at[up2(yh, dyh), :, up2(c, dc), :, columns]
                if dyh + dt + dc == 0:
                    stay = links.keep(src, ge.at[slot])
                else:
                    index = (dyh * 2 + dt) * 2 + dc
                    back.append(
                        links.send(src, ge.at[slot], expert_sems.at[index], links.flip(dyh=dyh, dt=dt, dc=dc))
                    )
    for copy in back:
        copy.wait_recv()
    stay.wait()
    links.finish()


def reduce_experts(g, gx):
    return pl.pallas_call(
        reduce_experts_kernel,
        out_shape=(
            jax.ShapeDtypeStruct((8, 3, 24, 384), BF),
            jax.ShapeDtypeStruct((OWN, D), F32),
        ),
        in_specs=[ANY] * 2,
        out_specs=(ANY, VMEM),
        scratch_shapes=[
            pltpu.VMEM((2, 3, 4, 2, 24, 768), BF),
            pltpu.VMEM((2, 3, 3, 4, 2, 24, 768), BF),
            pltpu.VMEM((2, 4, 3, 2, 24, 768), BF),
            pltpu.VMEM((2, 3, 3, 2, 24, 768), BF),
            pltpu.VMEM((2, 3, 2, 24, 768), BF),
        ]
        + TokenSum.SCRATCH
        + [pltpu.SemaphoreType.DMA((n,)) for n in (32, 8, 6, 6, 8)],
        compiler_params=pltpu.CompilerParams(
            collective_id=3, has_side_effects=True, vmem_limit_bytes=48 * MIB
        ),
        name="reduce_experts",
    )(g, gx)


def reduce_attention_kernel(
    g, mix, small, g_out, mix_out, small_out,
    own, twin, first, mid, second, last, ring,
    s_twin, s_one, s_first, s_two, s_second, s_three, s_ring,
    tok_own, tok_twin, tok_ring, tok_twin_sems, tok_ring_sems,
    send_sems, local_sems, twin_sems, first_sems, second_sems, ring_sems, small_sems,
):
    links = Links(send_sems, local_sems)
    yh, x, z, c, t = links.me
    links.barrier([links.at(**w) for w in ALONG + RING + [dict(dc=1)]])
    other = links.at(dc=1)
    order = (2, 1, 3, 0)

    def piece(h, k, core):
        return g.at[0, :, :, up4(z, k), core] if h == 0 else g.at[1, :, up4(x, k), :, core]

    s_copy = links.send(small, s_twin, small_sems.at[0], other)
    twins, kept = {}, {}
    for k in order:
        for h in (0, 1):
            twins[(h, k)] = links.send(piece(h, k, 1 - c), twin.at[h, k], twin_sems.at[h * 4 + k], other)
            kept[(h, k)] = links.keep(piece(h, k, c), own.at[h, k])
    tokens = TokenSum(links, mix, tok_own, tok_twin, tok_ring, tok_twin_sems, tok_ring_sems)
    s_copy.wait_recv()
    s_one[...] = small[...] + s_twin[...]
    s_copies = {}
    for k in (1, 2, 3):
        j = (4 - k) % 4
        s_copies[j] = links.send(s_one.at[:, up4(z, k)], s_first.at[j - 1], small_sems.at[j], links.at(dz=k))
    arrive = {}
    for k in order:
        for h in (0, 1):
            kept[(h, k)].wait()
            twins[(h, k)].wait_recv()
            for i in range(2):
                add_blocks([own.at[h, k, i], twin.at[h, k, i]], own.at[h, k, i], 4)
            if k:
                j = (4 - k) % 4
                target = links.at(dz=k) if h == 0 else links.at(dx=k)
                arrive[(h, j)] = links.send(
                    own.at[h, k], first.at[h, j - 1], first_sems.at[h * 3 + j - 1], target
                )
    tokens.spread()
    for j in (1, 2, 3):
        s_copies[j].wait_recv()
    s_two[...] = s_one[:, z] + s_first[0] + s_first[1] + s_first[2]
    for k in (1, 2, 3):
        j = (4 - k) % 4
        s_copies[j] = links.send(s_two.at[up4(x, k)], s_second.at[j - 1], small_sems.at[3 + j], links.at(dx=k))
    for j in (1, 3, 2):
        for h in (0, 1):
            arrive[(h, j)].wait_recv()
    final = {}
    for k in order:
        for h in (0, 1):
            place_of = up4(x, k) if h == 0 else up4(z, k)

            def body(i, carry):
                part = own[h, 0, i, place_of].astype(F32)
                for j in range(3):
                    part = part + first[h, j, i, place_of].astype(F32)
                mid[h, k, i] = part.astype(BF)
                return carry

            lax.fori_loop(0, 2, body, 0)
            if k:
                j = (4 - k) % 4
                target = links.at(dx=k) if h == 0 else links.at(dz=k)
                final[(h, j)] = links.send(
                    mid.at[h, k], second.at[h, j - 1], second_sems.at[h * 3 + j - 1], target
                )
    for j in (1, 2, 3):
        s_copies[j].wait_recv()
    s_three[...] = s_two[x] + s_second[0] + s_second[1] + s_second[2]
    for k in (1, 2, 3):
        j = (4 - k) % 4
        s_copies[j] = links.send(s_three, s_ring.at[j - 1], small_sems.at[6 + j], links.at(dy=k))
    tokens.total(mix_out)
    for h in (0, 1):
        for j in (1, 3, 2):
            final[(h, j)].wait_recv()
        add_blocks([mid.at[h, 0], second.at[h, 0], second.at[h, 1], second.at[h, 2]], last.at[h], 2)
    around = []
    for dyh, dt in ((1, 0), (0, 1), (1, 1)):
        index = dyh * 2 + dt - 1
        around.append(
            links.send(
                last.at[up2(t, dt), up2(yh, dyh)], ring.at[index], ring_sems.at[index], links.flip(dyh=dyh, dt=dt)
            )
        )
    for j in (1, 2, 3):
        s_copies[j].wait_recv()
    small_out[...] = s_three[...] + s_ring[0] + s_ring[1] + s_ring[2]
    for copy in around:
        copy.wait_recv()
    total = last[t, yh].astype(F32)
    for j in range(3):
        total = total + ring[j].astype(F32)
    g_out[...] = total
    links.finish()


def reduce_attention(g, mix, small):
    return pl.pallas_call(
        reduce_attention_kernel,
        out_shape=(
            jax.ShapeDtypeStruct((24, ATT), F32),
            jax.ShapeDtypeStruct((OWN, D), F32),
            jax.ShapeDtypeStruct((8, 128), F32),
        ),
        in_specs=[ANY, ANY, VMEM],
        out_specs=(VMEM, VMEM, VMEM),
        scratch_shapes=[
            pltpu.VMEM((2, 4, 2, 4, 24, ATT), BF),
            pltpu.VMEM((2, 4, 2, 4, 24, ATT), BF),
            pltpu.VMEM((2, 3, 2, 4, 24, ATT), BF),
            pltpu.VMEM((2, 4, 2, 24, ATT), BF),
            pltpu.VMEM((2, 3, 2, 24, ATT), BF),
            pltpu.VMEM((2, 2, 24, ATT), BF),
            pltpu.VMEM((3, 24, ATT), BF),
            pltpu.VMEM((4, 4, 8, 128), F32),
            pltpu.VMEM((4, 4, 8, 128), F32),
            pltpu.VMEM((3, 4, 8, 128), F32),
            pltpu.VMEM((4, 8, 128), F32),
            pltpu.VMEM((3, 8, 128), F32),
            pltpu.VMEM((8, 128), F32),
            pltpu.VMEM((3, 8, 128), F32),
        ]
        + TokenSum.SCRATCH
        + [pltpu.SemaphoreType.DMA((n,)) for n in (48, 16, 8, 6, 6, 3, 10)],
        compiler_params=pltpu.CompilerParams(
            collective_id=4, has_side_effects=True, vmem_limit_bytes=56 * MIB
        ),
        name="reduce_attention",
    )(g, mix, small)


def rope_tables(first, length, head_size):
    half_size = head_size // 2
    frequency = ROPE_BASE ** (-(2.0 * jnp.arange(half_size, dtype=F32)) / head_size)
    position = (first + jnp.arange(length)).astype(F32)
    angles = position[:, None] * frequency[None, :]
    angles = jnp.concatenate([angles, angles], axis=1)
    return (jnp.cos(angles), jnp.sin(angles))


def rotate(values, cosine, sine_table):
    half_size = values.shape[-1] // 2
    turned = jnp.concatenate([-values[..., half_size:], values[..., :half_size]], axis=-1)
    return values * cosine[:, None, :] + turned * sine_table[:, None, :]


def unrotate(gradient, cosine, sine_table):
    half_size = gradient.shape[-1] // 2
    carried = gradient * sine_table[:, None, :]
    turned = jnp.concatenate([-carried[..., half_size:], carried[..., :half_size]], axis=-1)
    return gradient * cosine[:, None, :] - turned


def norm_forward(tokens, gain_vec):
    inverse = lax.rsqrt(jnp.mean(tokens * tokens, axis=1, keepdims=True) + NORM_EPSILON)
    return (tokens * inverse * gain_vec, inverse)


def norm_backward(tokens, inverse, gain_vec, gradient):
    scaled = gradient * gain_vec
    gain_grad = jnp.sum(gradient * tokens * inverse, axis=0)
    token_grad = inverse * scaled - tokens * inverse**3 * jnp.mean(
        scaled * tokens, axis=1, keepdims=True
    )
    return (token_grad, gain_grad)


def mm(a, b, dims):
    return lax.dot_general(a, b, (dims, ((), ())), preferred_element_type=F32)


def shards(
    tokens_in, routes, cotangent, attn_gain, query_proj, key_proj, value_proj, output_proj,
    ffn_gain, router_proj, expert_gate, expert_up, expert_down,
):
    yh, x, z, c, t = place()
    extra = jnp.concatenate(
        [router_proj, attn_gain[:, None], ffn_gain[:, None], jnp.zeros((24, WIDE - ATT - 10), BF)], axis=1
    )
    a_block = jnp.concatenate([query_proj, key_proj, value_proj, output_proj, extra], axis=1)
    e_block = jnp.stack([expert_gate, expert_up, expert_down]).transpose(2, 0, 1, 3)
    a_all, e_mine, tok_pair, cot_all = gather_attention(a_block, e_block, tokens_in, cotangent)

    weights = a_all.reshape(2, D, WIDE)
    router = weights[0, :, ATT : ATT + 8]
    gain_attn = weights[0, :, ATT + 8].astype(F32)
    gain_ffn = weights[0, :, ATT + 9].astype(F32)
    inputs = tokens_in.astype(F32)
    normed_own, inverse_attn = norm_forward(inputs, gain_attn)
    normed_own = normed_own.astype(BF)
    normed_pair = norm_forward(tok_pair.reshape(SEQ, D).astype(F32), gain_attn)[0].astype(BF)
    cos_own, sin_own = rope_tables(OWN * t, OWN, HD)
    cos_all, sin_all = rope_tables(0, SEQ, HD)
    allowed = (OWN * t + jnp.arange(OWN))[:, None] >= jnp.arange(SEQ)[None, :]
    scale = HD ** (-0.5)
    queries, keys, values, logs, attended = [], [], [], [], []
    branch = 0.0
    for j in range(2):
        w = weights[j]
        q = mm(normed_own, w[:, :HALF], ((1,), (0,))).reshape(OWN, 6, HD)
        k = mm(normed_pair, w[:, HALF : HALF + HD], ((1,), (0,))).reshape(SEQ, 1, HD)
        v = mm(normed_pair, w[:, HALF + HD : QKV], ((1,), (0,))).astype(BF)
        q = rotate(q, cos_own, sin_own).astype(BF)
        k = rotate(k, cos_all, sin_all).astype(BF).reshape(SEQ, HD)
        scores = jnp.einsum("qgd,sd->gqs", q, k, preferred_element_type=F32) * scale
        scores = jnp.where(allowed[None], scores, -1e30)
        row_max = jnp.max(scores, axis=-1, keepdims=True)
        shifted = jnp.exp(scores - row_max)
        row_total = jnp.sum(shifted, axis=-1, keepdims=True)
        probs = (shifted / row_total).astype(BF)
        att = jnp.einsum("gqs,sd->qgd", probs, v, preferred_element_type=F32).astype(BF).reshape(OWN, HALF)
        branch = branch + mm(att, w[:, QKV:ATT], ((1,), (1,)))
        queries.append(q)
        keys.append(k)
        values.append(v)
        logs.append(row_max + jnp.log(row_total))
        attended.append(att)
    residual = inputs + branch
    normed_ffn, inverse_ffn = norm_forward(residual, gain_ffn)
    normed_ffn = normed_ffn.astype(BF)
    logits = mm(normed_ffn, router, ((1,), (0,)))
    own_routes = lax.dynamic_slice(routes, (OWN * t, 0), (OWN, 4))
    chosen = jnp.any(own_routes[:, :, None] == jnp.arange(E)[None, None, :], axis=1)
    masked = jnp.where(chosen, logits, -1e30)
    raised = jnp.where(chosen, jnp.exp(masked - jnp.max(masked, axis=1, keepdims=True)), 0.0)
    gates_own = raised / jnp.sum(raised, axis=1, keepdims=True)
    e_all, tok_all, gates_all = gather_experts(e_mine, normed_ffn, gates_own.T)

    rows = 8 * OWN
    experts = e_all.reshape(3, D, 768)
    tokens = tok_all.reshape(rows, D)
    cots = cot_all.reshape(rows, D)
    gates = gates_all.transpose(0, 1, 3, 2).reshape(rows, E)
    mine = (jnp.arange(E) == (yh * 2 + t) * 2 + c).astype(F32)
    gate = jnp.sum(gates * mine[None, :], axis=1, keepdims=True)
    gate_in = mm(tokens, experts[0], ((1,), (0,)))
    up_in = mm(tokens, experts[1], ((1,), (0,)))
    back = mm(cots, experts[2], ((1,), (0,)))
    sig = jax.nn.sigmoid(gate_in)
    act = gate_in * sig
    hidden = act * up_in
    grad_gate = jnp.sum(hidden * back, axis=1, keepdims=True)
    grad_logits = (gate * grad_gate * (mine[None, :] - gates)).astype(BF)
    weighted = (gate * hidden).astype(BF)
    grad_hidden = gate * back
    grad_gate_in = (grad_hidden * up_in * sig * (1.0 + gate_in * (1.0 - sig))).astype(BF)
    grad_up_in = (grad_hidden * act).astype(BF)
    mixture = mm(weighted, experts[2], ((1,), (1,))).astype(BF)
    grad_tokens = (
        mm(grad_gate_in, experts[0], ((1,), (1,)))
        + mm(grad_up_in, experts[1], ((1,), (1,)))
        + mm(grad_logits, router, ((1,), (1,)))
    ).astype(BF)
    grad_experts = jnp.stack(
        [
            mm(tokens, grad_gate_in, ((0,), (0,))).astype(BF),
            mm(tokens, grad_up_in, ((0,), (0,))).astype(BF),
            mm(cots, weighted, ((0,), (0,))).astype(BF),
        ]
    )
    grad_router = mm(tokens, grad_logits, ((0,), (0,)))
    ge, grad_normed_ffn = reduce_experts(
        grad_experts.reshape(3, 2, 4, 4, 2, 24, 768), grad_tokens.reshape(4, 2, OWN, D)
    )
    ge = ge.astype(F32).transpose(1, 2, 0, 3)

    grad_norm, grad_gain_ffn = norm_backward(residual, inverse_ffn, gain_ffn, grad_normed_ffn)
    grad_residual = cotangent.astype(F32) + grad_norm
    grad_branch = grad_residual.astype(BF)
    grad_q, grad_k, grad_v, grad_o = [], [], [], []
    for j in range(2):
        w = weights[j]
        q, k, v = queries[j], keys[j], values[j]
        grad_att = mm(grad_branch, w[:, QKV:ATT], ((1,), (0,))).astype(BF).reshape(OWN, 6, HD)
        scores = jnp.einsum("qgd,sd->gqs", q, k, preferred_element_type=F32) * scale
        scores = jnp.where(allowed[None], scores, -1e30)
        exact = jnp.exp(scores - logs[j])
        probs = exact.astype(BF)
        grad_probs = jnp.einsum("qgd,sd->gqs", grad_att, v, preferred_element_type=F32)
        centred = jnp.sum(exact * grad_probs, axis=-1, keepdims=True)
        grad_scores = (exact * (grad_probs - centred)).astype(BF)
        grad_q.append(jnp.einsum("gqs,sd->qgd", grad_scores, k, preferred_element_type=F32) * scale)
        grad_k.append(jnp.einsum("gqs,qgd->sd", grad_scores, q, preferred_element_type=F32) * scale)
        grad_v.append(jnp.einsum("gqs,qgd->sd", probs, grad_att, preferred_element_type=F32))
        grad_o.append(mm(grad_branch, attended[j], ((0,), (0,))).astype(BF))
    grad_kv = jnp.concatenate([grad_k[0], grad_k[1], grad_v[0], grad_v[1]], axis=1)
    theirs = lax.dynamic_slice(grad_kv, (OWN * (1 - t), 0), (OWN, 4 * HD)).astype(BF)
    received = lax.ppermute(theirs, "tensor", [(0, 1), (1, 0)])
    grad_kv = lax.dynamic_slice(grad_kv, (OWN * t, 0), (OWN, 4 * HD)) + received.astype(F32)
    grad_normed = 0.0
    grad_a = []
    for j in range(2):
        w = weights[j]
        gq = unrotate(grad_q[j], cos_own, sin_own).astype(BF).reshape(OWN, HALF)
        gk = unrotate(grad_kv[:, HD * j : HD * (j + 1)].reshape(OWN, 1, HD), cos_own, sin_own)
        gk = gk.astype(BF).reshape(OWN, HD)
        gv = grad_kv[:, HD * (2 + j) : HD * (3 + j)].astype(BF)
        lin = jnp.concatenate([gq, gk, gv], axis=1)
        grad_normed = grad_normed + mm(lin, w[:, :QKV], ((1,), (1,)))
        grad_a.append(jnp.concatenate([mm(normed_own, lin, ((0,), (0,))).astype(BF), grad_o[j]], axis=1))
    grad_input_norm, grad_gain_attn = norm_backward(inputs, inverse_attn, gain_attn, grad_normed)
    grad_input = (grad_residual + grad_input_norm).astype(BF)

    small = jnp.concatenate([grad_router, grad_gain_attn[:, None], grad_gain_ffn[:, None]], axis=1)
    small = small.reshape(2, 4, 4, 2, 24, 10).transpose(1, 2, 0, 3, 4, 5).reshape(16, 960)
    small = jnp.pad(small, ((0, 0), (0, 64))).reshape(4, 4, 8, 128)
    ga, mix, small = reduce_attention(
        jnp.stack(grad_a).reshape(2, 2, 4, 4, 2, 24, ATT), mixture.reshape(4, 2, OWN, D), small
    )
    layer_output = (residual + mix).astype(BF)
    small = small.reshape(1024)[:960].reshape(2, 2, 2, 12, 10)
    small = lax.dynamic_slice(small, (yh, c, t, 0, 0), (1, 1, 1, 12, 10)).reshape(12, 10)
    return (
        layer_output,
        grad_input,
        small[:, 8],
        ga[:, :HALF],
        ga[:, HALF : HALF + HD],
        ga[:, HALF + HD : QKV],
        ga[:, QKV:],
        small[:, 9],
        small[:, :8],
        ge[0],
        ge[1],
        ge[2],
    )


def solution(mesh):
    return jax.shard_map(
        shards,
        mesh=mesh,
        in_specs=(
            P(("dp", "tensor"), None),
            P("dp", None),
            P(("dp", "tensor"), None),
            P("dp"),
            P("dp", "tensor"),
            P("dp", "tensor"),
            P("dp", "tensor"),
            P("dp", "tensor"),
            P("dp"),
            P("dp", None),
            P("dp", None, "tensor"),
            P("dp", None, "tensor"),
            P("dp", None, "tensor"),
        ),
        out_specs=(
            P(("dp", "tensor"), None),
            P(("dp", "tensor"), None),
            P(("dp", "tensor")),
            P("dp", "tensor"),
            P("dp", "tensor"),
            P("dp", "tensor"),
            P("dp", "tensor"),
            P(("dp", "tensor")),
            P(("dp", "tensor"), None),
            P("dp", None, "tensor"),
            P("dp", None, "tensor"),
            P("dp", None, "tensor"),
        ),
        check_vma=False,
    )
```

time: 2360 us -> 540 us (0.23)
  waiting for transfers between devices: 1320 us -> 0.01 us
  blocking collectives: 517 us -> 0 us
  Pallas kernels: 0 us -> 253 us
  local copies, waits for them, and re-layouts: 223 us -> 69.8 us
  other arithmetic: 94.2 us -> 59.4 us
  matrix products: 171 us -> 146 us
    reduce_scatter x9 -> x0, waiting for transfers between devices: 1020 us -> none  [the longest x1 222 us: shards(): lax.psum_scatter(grad_gate_w, 'dp', scatter_dimension=0, tiled=True)]
    all_gather x3 -> x0, blocking collectives: 277 us -> none  [the longest x1 96.2 us: shards(): lax.all_gather(router_proj, 'dp', axis=0, tiled=True)]
    pallas_call x0 -> x4, Pallas kernels: none -> 253 us  [the longest x1 71.2 us: gather_attention(): pl.pallas_call(gather_attention_kernel, out_shape=(jax.ShapeDtypeStruct((...]
    unnamed x2 -> x0, blocking collectives: 240 us -> none
    all_gather x9 -> x0, waiting for transfers between devices: 152 us -> none  [the longest x1 72.8 us: shards(): lax.all_gather(expert_down, 'dp', axis=0, tiled=True)]
    unnamed x22 -> x0, waiting for transfers between devices: 148 us -> none
    gather x9 -> x0, local copies, waits for them, and re-layouts: 71.9 us -> none  [the longest x1 19.9 us: shards(): jnp.take(expert_out, slot_index, axis=0).reshape(length, TOP, model_width)]
    transpose x3 -> x1, local copies, waits for them, and re-layouts: 56.9 us -> 0.45 us  [shards(): small.reshape(2, 4, 4, 2, 24, 10).transpose(1, 2, 0, 3, 4, 5)]
  transfers between devices with their start and end apart: 20 -> 1, of which waited for: 11 -> 0; matrix products, arithmetic and copies ran while one was open for 12% -> 4% of each run, Pallas kernels for 0% -> 0%
where the time goes in v1:
time: 540 us; the launch traced here: 531 us
  Pallas kernels  253 us (47%)
  matrix products  146 us (27%)
  local copies, waits for them, and re-layouts  69.8 us (13%)
  other arithmetic  59.4 us (11%)
    dot_general x28, matrix products, mm(): return lax.dot_general(a, b, (dims, ((), ())), preferred_element_type=F32)  129 us
    pallas_call x1, Pallas kernels, gather_attention(): pl.pallas_call(gather_attention_kernel, out_shape=(jax.ShapeDtypeStruct((...  71.2 us
    pallas_call x1, Pallas kernels, reduce_experts(): pl.pallas_call(reduce_experts_kernel, out_shape=(jax.ShapeDtypeStruct((8,...  62.7 us
    pallas_call x1, Pallas kernels, reduce_attention(): pl.pallas_call(reduce_attention_kernel, out_shape=(jax.ShapeDtypeStruct((...  59.8 us
    pallas_call x1, Pallas kernels, gather_experts(): pl.pallas_call(gather_experts_kernel, out_shape=(jax.ShapeDtypeStruct((3,...  59.4 us
    unnamed x150, local copies, waits for them, and re-layouts  17 us
    concatenate x2, local copies, waits for them, and re-layouts, shards(): jnp.concatenate([mm(normed_own, lin, ((0,), (0,))).astype(BF), grad_o[j]]...  16.1 us
  transfers between devices with their start and end apart: 1, of which 0 were waited for; matrix products, arithmetic and copies ran while one was open for 4% of the time, Pallas kernels for 0%

profile of v1, /device:TPU:0, one launch (start us, length us, event | category | flops | bytes accessed | tf_op | source)
XLA Modules:
  0.0 530.9 jit_solution(5864985738069228470)
XLA Ops:
  8.7 71.2 %gather_attention.1 = (bf16[2,2,4,4,2,24,1920]{6,5,4,3,2,1,0:T(8,128)(2,1)}, bf16[3,2,2,24,768]{4,3,2,1,0:T(8,128)(2,1)}, bf16[2,256,1536]{2,1,0:T(8,128)(2,1)}, bf16[4,2,256,1536]{3,2,1,0:T(8,128)(2,1)}) custom-call(bf16[24,1920]{1,0:T(8,128)(2,1)} %concatenate.88.a, bf16[8,3,24,384]{3,2,1,0:T(8,128)(2,1)} %maximum_bitcast_fusion.e, bf16[256,1536]{1,0:T(8,128)(2,1)} %tok.1, ...), custom_call_target="tpu_custom_call" | custom-call | tf_op jit(solution)/shard_map/gather_attention/pallas_call | solution.py:197
  79.9 1.8 multiply_reduce_fusion.1
  81.7 9.9 %fusion.119 = (bf16[1,2,4,4,2,24,1920]{6,5,4,3,2,1,0:T(8,128)(2,1)}, bf16[1,2,4,4,2,24,1920]{6,5,4,3,2,1,0:T(8,128)(2,1)}) fusion(bf16[2,2,4,4,2,24,1920]{6,5,4,3,2,1,0:T(8,128)(2,1)} %get-tuple-element.25), kind=kLoop, calls=%fused_computation.229 | loop fusion | bytes 23592960 | tf_op jit(solution)/shard_map/slice | solution.py:632
  91.7 2.1 fusion.118
  94.5 2.4 fusion.65
  96.9 1.7 fusion.72
  101.8 2.5 fusion.22
  112.2 1.7 fusion.88
  116.6 1.7 copy.206
  118.5 2.9 add_convert_fusion.4
  123.8 2.3 fusion.87
  128.5 2.6 fusion.29
  133.5 2.8 multiply_reduce_fusion.4
  138.8 59.4 %gather_experts.1 = (bf16[3,2,4,4,2,24,768]{6,5,4,3,2,1,0:T(8,128)(2,1)}, bf16[4,2,256,1536]{3,2,1,0:T(8,128)(2,1)}, f32[4,2,8,256]{3,2,1,0:T(8,128)}) custom-call(bf16[3,2,2,24,768]{4,3,2,1,0:T(8,128)(2,1)} %get-tuple-element.26.e_mine, bf16[256,1536]{1,0:T(8,128)(2,1)} %copy-done.22, f32[8,256]{1,0:T(8,128)} %fusion.105.gates), custom_call_target="tpu_custom_call" | custom-call | tf_op jit(solution)/shard_map/gather_experts/pallas_call | solution.py:253
  198.3 5.3 %fusion.120 = (bf16[1,2,4,4,2,24,768]{6,5,4,3,2,1,0:T(8,128)(2,1)}, bf16[1,2,4,4,2,24,768]{6,5,4,3,2,1,0:T(8,128)(2,1)S(1)}, bf16[1,2,4,4,2,24,768]{6,5,4,3,2,1,0:T(8,128)(2,1)S(1)}) fusion(bf16[3,2,4,4,2,24,768]{6,5,4,3,2,1,0:T(8,128)(2,1)} %get-tuple-element.30), kind=kLoop, calls=%fused_computation.230 | loop fusion | bytes 14155776 | tf_op jit(solution)/shard_map/slice | solution.py:671
  203.7 7.2 %fusion.127 = f32[2048,768]{0,1:T(8,128)} fusion(bf16[2048,1536]{1,0:T(8,128)(2,1)S(1)} %bitcast.249, bf16[1536,768]{1,0:T(8,128)(2,1)S(1)} %bitcast.275), kind=kOutput, calls=%fused_computation.237 | convolution fusion | flops 4831838208 | bytes 14942208 | tf_op jit(solution)/shard_map/dot_general | solution.py:602
  211.0 7.2 %fusion.126 = f32[2048,768]{0,1:T(8,128)} fusion(bf16[2048,1536]{1,0:T(8,128)(2,1)S(1)} %bitcast.250, bf16[1536,768]{1,0:T(8,128)(2,1)S(1)} %bitcast.277), kind=kOutput, calls=%fused_computation.236 | convolution fusion | flops 4831838208 | bytes 14942208 | tf_op jit(solution)/shard_map/dot_general | solution.py:602
  218.2 16.8 %multiply_reduce_fusion = (f32[2048]{0:T(1024)S(1)}, bf16[2048,768]{0,1:T(8,128)(2,1)}, bf16[2048,768]{0,1:T(8,128)(2,1)}, bf16[2048,768]{0,1:T(8,128)(2,1)}) fusion(f32[2048,768]{0,1:T(8,128)} %fusion.126, f32[2048,768]{0,1:T(8,128)} %fusion.127, f32[2048]{0:T(1024)S(1)} %bitcast.299, bf16[2048,1536]{1,0:T(8,128)(2,1)} %bitcast.304, ...), kind=kOutput, calls=%fused_computation.4 | convolution fusion | flops 4861720576 | bytes 30687232 | tf_op jit(solution)/shard_map/dot_general | solution.py:602
  235.0 8.5 %convolution_convert_fusion.6 = bf16[1536,768]{1,0:T(8,128)(2,1)} fusion(bf16[2048,1536]{1,0:T(8,128)(2,1)S(1)} %bitcast.251, bf16[2048,768]{0,1:T(8,128)(2,1)} %get-tuple-element.109), kind=kOutput, calls=%fused_computation.23 | convolution fusion | flops 4833017856 | bytes 11796480 | tf_op jit(solution)/shard_map/dot_general | solution.py:602
  243.5 8.2 %fusion.129 = f32[2048,1536]{1,0:T(8,128)} fusion(bf16[2048,768]{0,1:T(8,128)(2,1)S(1)} %copy-done.60, bf16[1536,768]{1,0:T(8,128)(2,1)S(1)} %bitcast.278), kind=kOutput, calls=%fused_computation.239 | convolution fusion | flops 4831838208 | bytes 18087936 | tf_op jit(solution)/shard_map/dot_general | solution.py:602
  251.7 6.6 %convolution_convert_fusion.7 = bf16[1536,768]{1,0:T(8,128)(2,1)} fusion(bf16[2048,1536]{1,0:T(8,128)(2,1)S(1)} %bitcast.252, bf16[2048,768]{0,1:T(8,128)(2,1)S(1)} %copy-done.59), kind=kOutput, calls=%fused_computation.24 | convolution fusion | flops 4833017856 | bytes 11796480 | tf_op jit(solution)/shard_map/dot_general | solution.py:602
  258.3 8.2 %fusion.128 = f32[2048,1536]{1,0:T(8,128)} fusion(bf16[2048,768]{0,1:T(8,128)(2,1)S(1)} %copy-done.59, bf16[1536,768]{1,0:T(8,128)(2,1)S(1)} %bitcast.276), kind=kOutput, calls=%fused_computation.238 | convolution fusion | flops 4831838208 | bytes 18087936 | tf_op jit(solution)/shard_map/dot_general | solution.py:602
  266.5 6.4 %convolution_convert_fusion.5 = bf16[1536,768]{1,0:T(8,128)(2,1)} fusion(bf16[2048,1536]{1,0:T(8,128)(2,1)S(1)} %bitcast.307, bf16[2048,768]{0,1:T(8,128)(2,1)S(1)} %copy-done.61), kind=kOutput, calls=%fused_computation.22 | convolution fusion | flops 4833017856 | bytes 11796480 | tf_op jit(solution)/shard_map/dot_general | solution.py:602
  273.0 6.4 %pad_maximum_fusion.1.g = bf16[3,2,4,4,2,24,768]{6,5,4,3,2,1,0:T(8,128)(2,1)} fusion(bf16[1,2,4,4,2,24,768]{6,5,4,3,2,1,0:T(8,128)(2,1)} %bitcast.281, bf16[1,2,4,4,2,24,768]{6,5,4,3,2,1,0:T(8,128)(2,1)} %bitcast.279, bf16[1,2,4,4,2,24,768]{6,5,4,3,2,1,0:T(8,128)(2,1)} %bitcast.280), kind=kLoop, calls=%fused_computation.3 | loop fusion | flops 7077888 | bytes 14155776 | tf_op jit(solution)/shard_map/stack | solution.py:687
  279.4 12.1 %add_convert_fusion = bf16[2048,1536]{1,0:T(8,128)(2,1)} fusion(f32[2048,1536]{1,0:T(8,128)} %fusion.128, f32[2048,1536]{1,0:T(8,128)} %fusion.129, bf16[2048,8]{0,1:T(8,128)(2,1)S(1)} %bitcast.295, bf16[2,1536,1920]{2,1,0:T(8,128)(2,1)} %bitcast.240), kind=kOutput, calls=%fused_computation | convolution fusion | flops 59768832 | bytes 31883264 | tf_op jit(solution)/shard_map/dot_general | solution.py:602
  291.6 62.7 %reduce_experts.1 = (bf16[8,3,24,384]{3,2,1,0:T(8,128)(2,1)S(1)}, f32[256,1536]{1,0:T(8,128)S(1)}) custom-call(bf16[3,2,4,4,2,24,768]{6,5,4,3,2,1,0:T(8,128)(2,1)} %pad_maximum_fusion.1.g, bf16[4,2,256,1536]{3,2,1,0:T(8,128)(2,1)} %bitcast.235), custom_call_target="tpu_custom_call" | custom-call | tf_op jit(solution)/shard_map/reduce_experts/pallas_call | solution.py:404
  355.5 1.7 fusion.117
  357.1 3.2 fusion.54
  360.3 3.2 fusion.51
  364.7 3.4 fusion.57
  368.2 2.3 fusion.8
  371.7 3.4 fusion.60
  386.1 3.8 convolution_bitcast_fusion
  390.5 7.4 %convolution_convert_fusion = bf16[2048,1536]{1,0:T(8,128)(2,1)} fusion(bf16[2048,768]{0,1:T(8,128)(2,1)S(1)} %copy-done.62, bf16[1536,768]{1,0:T(8,128)(2,1)S(1)} %bitcast.274), kind=kOutput, calls=%fused_computation.2 | convolution fusion | flops 4834983936 | bytes 11796480 | tf_op jit(solution)/shard_map/dot_general | solution.py:602
  397.9 2.2 convolution_convert_fusion.4
  400.1 2.2 convolution_convert_fusion.3
  406.1 1.9 convolution_bitcast_fusion.1
  414.2 2.8 convolution_convert_fusion.1
  417.0 2.7 convolution_convert_fusion.2
  419.8 2.5 fusion.44
  424.0 5.4 %pad_maximum_fusion.2 = bf16[1536,1792]{0,1:T(8,128)(2,1)} fusion(bf16[1536,768]{0,1:T(8,128)(2,1)} %convolution_convert_fusion.4, bf16[1536,1024]{0,1:T(8,128)(2,1)} %convolution_convert_fusion.2), kind=kLoop, calls=%fused_computation.10 | loop fusion | flops 11010048 | bytes 11010048 | tf_op jit(solution)/shard_map/concatenate | solution.py:733
  429.4 8.0 %copy.230 = bf16[1536,1792]{1,0:T(8,128)(2,1)} copy(bf16[1536,1792]{0,1:T(8,128)(2,1)} %pad_maximum_fusion.2) | data formatting | bytes 11010048 | tf_op jit(solution)/shard_map/concatenate | solution.py:733
  437.4 5.4 %pad_maximum_fusion.3 = bf16[1536,1792]{0,1:T(8,128)(2,1)} fusion(bf16[1536,768]{0,1:T(8,128)(2,1)} %convolution_convert_fusion.3, bf16[1536,1024]{0,1:T(8,128)(2,1)} %convolution_convert_fusion.1), kind=kLoop, calls=%fused_computation.11 | loop fusion | flops 11010048 | bytes 11010048 | tf_op jit(solution)/shard_map/concatenate | solution.py:733
  442.8 8.0 %copy.232 = bf16[1536,1792]{1,0:T(8,128)(2,1)} copy(bf16[1536,1792]{0,1:T(8,128)(2,1)} %pad_maximum_fusion.3) | data formatting | bytes 11010048 | tf_op jit(solution)/shard_map/concatenate | solution.py:733
  450.9 9.6 %pad_maximum_fusion.g = bf16[2,2,4,4,2,24,1792]{6,5,4,3,2,1,0:T(8,128)(2,1)} fusion(bf16[1,2,4,4,2,24,1792]{6,5,4,3,2,1,0:T(8,128)(2,1)} %bitcast.237, bf16[1,2,4,4,2,24,1792]{6,5,4,3,2,1,0:T(8,128)(2,1)} %bitcast.236), kind=kLoop, calls=%fused_computation.1 | loop fusion | flops 5505024 | bytes 22020096 | tf_op jit(solution)/shard_map/stack | solution.py:741
  460.5 59.8 %reduce_attention.1 = (f32[24,1792]{1,0:T(8,128)}, f32[256,1536]{1,0:T(8,128)}, f32[8,128]{1,0:T(8,128)}) custom-call(bf16[2,2,4,4,2,24,1792]{6,5,4,3,2,1,0:T(8,128)(2,1)} %pad_maximum_fusion.g, bf16[4,2,256,1536]{3,2,1,0:T(8,128)(2,1)} %bitcast.267, f32[4,4,8,128]{3,2,1,0:T(8,128)} %bitcast.296), custom_call_target="tpu_custom_call" | custom-call | tf_op jit(solution)/shard_map/reduce_attention/pallas_call | solution.py:531
  523.2 2.6 add_convert_fusion.1
  527.3 3.2 fusion.43
  (248 shorter events, 63.0 us)
Async XLA Ops:
  0.6 105.1 %copy-start = (s32[512,4]{0,1:T(4,128)S(1)}, s32[512,4]{0,1:T(4,128)}, u32[]{:S(2)}) copy-start(s32[512,4]{0,1:T(4,128)} %param.14) | copy-start | bytes 24580
  81.7 12.3 %copy-start.23 = (bf16[2,256,1536]{2,1,0:T(8,128)(2,1)S(1)}, bf16[2,256,1536]{2,1,0:T(8,128)(2,1)}, u32[]{:S(2)}) copy-start(bf16[2,256,1536]{2,1,0:T(8,128)(2,1)} %get-tuple-element.24) | copy-start | bytes 4718596
  94.0 10.3 %copy-start.51 = (f32[1536]{0:T(1024)}, f32[1536]{0:T(1024)S(1)}, u32[]{:S(2)}) copy-start(f32[1536]{0:T(1024)S(1)} %convert_reduce_fusion.1) | copy-start | bytes 18436
  94.1 4.6 copy-start.10
  96.9 4.9 copy-start.11
  101.8 2.5 copy-start.55
  104.3 9.9 %copy-start.26 = (f32[256,768]{1,0:T(8,128)}, f32[256,768]{1,0:T(8,128)S(1)}, u32[]{:S(2)}) copy-start(f32[256,768]{1,0:T(8,128)S(1)} %fusion.22) | copy-start | bytes 2359300
  105.2 8.7 %copy-start.27 = (f32[256,768]{1,0:T(8,128)}, f32[256,768]{1,0:T(8,128)S(1)}, u32[]{:S(2)}) copy-start(f32[256,768]{1,0:T(8,128)S(1)} %fusion.20) | copy-start | bytes 2359300
  114.2 2.3 copy-start.15
  116.5 4.9 copy-start.19
  126.1 5.1 copy-start.41
  128.5 3.3 copy-start.45
  133.5 2.8 copy-start.37
  133.5 3.0 copy-start.53
  136.5 2.3 copy-start.22
  198.2 5.4 %copy-start.47 = (f32[4,2,8,256]{3,2,1,0:T(8,128)S(1)}, f32[4,2,8,256]{3,2,1,0:T(8,128)}, u32[]{:S(2)}) copy-start(f32[4,2,8,256]{3,2,1,0:T(8,128)} %get-tuple-element.28) | copy-start | bytes 196612
  198.2 5.4 %copy-start.58 = (f32[8]{0:T(128)S(1)}, f32[8]{0:T(128)}, u32[]{:S(2)}) copy-start(f32[8]{0:T(128)} %compare_convert_fusion) | copy-start | bytes 100
  198.3 5.5 %copy-start.14 = (bf16[4,2,256,1536]{3,2,1,0:T(8,128)(2,1)S(1)}, bf16[4,2,256,1536]{3,2,1,0:T(8,128)(2,1)}, u32[]{:S(2)}) copy-start(bf16[4,2,256,1536]{3,2,1,0:T(8,128)(2,1)} %get-tuple-element.27) | copy-start | bytes 18874372
  203.6 7.4 %copy-start.29 = (bf16[1,2,4,4,2,24,768]{6,5,4,3,2,1,0:T(8,128)(2,1)}, bf16[1,2,4,4,2,24,768]{6,5,4,3,2,1,0:T(8,128)(2,1)S(1)}, u32[]{:S(2)}) copy-start(bf16[1,2,4,4,2,24,768]{6,5,4,3,2,1,0:T(8,128)(2,1)S(1)} %get-tuple-element.115) | copy-start | bytes 7077892
  203.6 7.4 %copy-start.31 = (bf16[1,2,4,4,2,24,768]{6,5,4,3,2,1,0:T(8,128)(2,1)}, bf16[1,2,4,4,2,24,768]{6,5,4,3,2,1,0:T(8,128)(2,1)S(1)}, u32[]{:S(2)}) copy-start(bf16[1,2,4,4,2,24,768]{6,5,4,3,2,1,0:T(8,128)(2,1)S(1)} %get-tuple-element.116) | copy-start | bytes 7077892
  235.0 8.5 %copy-start.32 = (bf16[1,2,4,4,2,24,768]{6,5,4,3,2,1,0:T(8,128)(2,1)S(1)}, bf16[1,2,4,4,2,24,768]{6,5,4,3,2,1,0:T(8,128)(2,1)}, u32[]{:S(2)}) copy-start(bf16[1,2,4,4,2,24,768]{6,5,4,3,2,1,0:T(8,128)(2,1)} %copy-done.31) | copy-start | bytes 7077892
  235.0 8.5 %copy-start.60 = (bf16[2048,768]{0,1:T(8,128)(2,1)S(1)}, bf16[2048,768]{0,1:T(8,128)(2,1)}, u32[]{:S(2)}) copy-start(bf16[2048,768]{0,1:T(8,128)(2,1)} %get-tuple-element.109) | copy-start | bytes 9437188
  243.5 8.2 %copy-start.59 = (bf16[2048,768]{0,1:T(8,128)(2,1)S(1)}, bf16[2048,768]{0,1:T(8,128)(2,1)}, u32[]{:S(2)}) copy-start(bf16[2048,768]{0,1:T(8,128)(2,1)} %get-tuple-element.107) | copy-start | bytes 9437188
  251.7 6.6 %copy-start.30 = (bf16[1,2,4,4,2,24,768]{6,5,4,3,2,1,0:T(8,128)(2,1)S(1)}, bf16[1,2,4,4,2,24,768]{6,5,4,3,2,1,0:T(8,128)(2,1)}, u32[]{:S(2)}) copy-start(bf16[1,2,4,4,2,24,768]{6,5,4,3,2,1,0:T(8,128)(2,1)} %copy-done.29) | copy-start | bytes 7077892
  251.7 14.8 %slice-start.4 = ((s8[6291456]{0:T(1024)(128)(4,1)}), s8[4194304]{0:T(1024)(128)(4,1)S(1)}, s32[]{:S(2)}) async-start(s8[6291456]{0:T(1024)(128)(4,1)} %bitcast.305), calls=%async_computation.4 | async-start | bytes 8388608
  258.3 8.2 %slice-start.5 = ((s8[6291456]{0:T(1024)(128)(4,1)}), s8[2097152]{0:T(1024)(128)(4,1)S(1)}, s32[]{:S(2)}) async-start(s8[6291456]{0:T(1024)(128)(4,1)} %bitcast.305), calls=%async_computation.5 | async-start | bytes 4194304
  258.3 8.2 %copy-start.61 = (bf16[2048,768]{0,1:T(8,128)(2,1)S(1)}, bf16[2048,768]{0,1:T(8,128)(2,1)}, u32[]{:S(2)}) copy-start(bf16[2048,768]{0,1:T(8,128)(2,1)} %get-tuple-element.108) | copy-start | bytes 9437188
  363.5 4.6 copy-start.50
  364.7 3.4 copy-start.3
  371.7 3.4 copy-start.6
  375.1 2.8 copy-start.13
  385.4 22.6 %collective-permute-start = (bf16[256,512]{0,1:T(8,128)(2,1)}, bf16[256,512]{0,1:T(8,128)(2,1)}, u32[]{:S(2)}, u32[]{:S(2)}) collective-permute-start(bf16[256,512]{0,1:T(8,128)(2,1)} %dynamic-slice_convert_fusion), channel_id=1, source_target_pairs={{0,1},{1,0},{2,3},{3,2},{4,5},{5,4},{6,7},{7,6},{8,9},{9,8},{10,11... | collective-permute-start | bytes 786440 | tf_op jit(solution)/shard_map/ppermute | solution.py:721
  386.1 3.8 copy-start.28
  386.1 4.4 copy-start.62
  390.5 7.4 %copy-start.46 = (bf16[128,6,256]{2,0,1:T(8,128)(2,1)S(1)}, bf16[128,6,256]{2,0,1:T(8,128)(2,1)}, u32[]{:S(2)}) copy-start(bf16[128,6,256]{2,0,1:T(8,128)(2,1)} %copy-done.45) | copy-start | bytes 1179652
  397.9 2.3 copy-start.38
  402.3 3.8 copy-start.42
  403.8 5.5 %copy-start.36 = (f32[256,64]{0,1:T(8,128)S(1)}, f32[256,64]{0,1:T(8,128)}, u32[]{:S(2)}) copy-start(f32[256,64]{0,1:T(8,128)} %copy-done.35) | copy-start | bytes 196612
  406.1 4.1 copy-start.8
  406.1 4.1 copy-start.40
  410.2 2.2 slice-start
  410.7 2.4 slice-start.1
  413.1 6.7 %slice-start.2 = ((s8[5898240]{0:T(1024)(128)(4,1)}), s8[1703936]{0:T(1024)(128)(4,1)S(1)}, s32[]{:S(2)}) async-start(s8[5898240]{0:T(1024)(128)(4,1)} %bitcast.264), calls=%async_computation.2 | async-start | bytes 3407872
  414.2 5.5 %slice-start.3 = ((s8[5898240]{0:T(1024)(128)(4,1)}), s8[4194304]{0:T(1024)(128)(4,1)S(1)}, s32[]{:S(2)}) async-start(s8[5898240]{0:T(1024)(128)(4,1)} %bitcast.264), calls=%async_computation.3 | async-start | bytes 8388608
  419.8 2.7 copy-start.43
  520.2 5.5 %copy-start.57 = (f32[8,128]{1,0:T(8,128)S(1)}, f32[8,128]{1,0:T(8,128)}, u32[]{:S(2)}) copy-start(f32[8,128]{1,0:T(8,128)} %get-tuple-element.33) | copy-start | bytes 12292
  520.2 7.0 %copy-start.54 = (f32[256]{0:T(256)S(1)}, f32[256]{0:T(256)}, u32[]{:S(2)}) copy-start(f32[256]{0:T(256)} %get-tuple-element.158) | copy-start | bytes 3076
  523.2 7.3 %copy-start.1 = (s32[512,4]{0,1:T(4,128)S(1)}, s32[512,4]{0,1:T(4,128)}, u32[]{:S(2)}) copy-start(s32[512,4]{0,1:T(4,128)} %param.14) | copy-start | bytes 24580
  (22 other events, 29.6 us)
